TPU v7x, 32 devices: a whole 2x2x4 slice. The times are simulated.
32 devices in a mesh: tr: 8 (over z, x), tc: 4 (over y, core).
Axes of the slice: x: 2, y: 2, z: 4, core: 2. Of those that a mesh axis runs over, the one named last changes fastest.
Arguments:
- frame_one: bfloat16 [16, 256, 128], P('tr', 'tc'), may hold values from -20 to 20
- frame_two: bfloat16 [16, 256, 128], P('tr', 'tc'), may hold values from -20 to 20
- first_kernel: bfloat16 [3, 3, 128, 128], replicated, may hold values from -0.1875 to 0.1875
- second_kernel: bfloat16 [3, 3, 128, 128], replicated, may hold values from -0.1875 to 0.1875
- out_proj: bfloat16 [128, 256], replicated, may hold values from -0.5 to 0.5
- out_bias: float32 [256], replicated, may hold values from -0.4 to 0.4
Outputs:
- corr_level1: bfloat16 [16, 256, 1024], P('tr', 'tc')
- corr_level2: bfloat16 [16, 256, 256], P('tr', 'tc')
- corr_level3: bfloat16 [16, 256, 64], P('tr', 'tc')
All inputs are finite; a program needn't handle non-finite values.
Results may differ from a plain program's by a relative error of at most 0.0035.
Values may be sent and summed in bfloat16 or wider, within the bound.
A program may use at most 64 MiB of HBM per device.

v0:
```python
import math

import jax
import jax.numpy as jnp
from jax import lax
from jax.sharding import PartitionSpec as P


def with_halo(block, sides, width):
    for axis, dim in sides:
        count = lax.axis_size(axis)
        forward = [(i, i + 1) for i in range(count - 1)]
        backward = [(target, source) for source, target in forward]
        low = lax.ppermute(
            lax.slice_in_dim(block, block.shape[dim] - width, None, axis=dim), axis, forward
        )
        high = lax.ppermute(lax.slice_in_dim(block, 0, width, axis=dim), axis, backward)
        block = jnp.concatenate([low, block, high], axis=dim)
    return block


def convolve(padded, kernel):
    out_rows = padded.shape[1] - 2
    out_cols = padded.shape[2] - 2
    summed = jnp.zeros((padded.shape[0], out_rows, out_cols, kernel.shape[3]), jnp.float32)
    for down_step in range(3):
        for side_step in range(3):
            window = padded[
                :, down_step : down_step + out_rows, side_step : side_step + out_cols, :
            ]
            summed = summed + jnp.einsum(
                "fhwc,cd->fhwd",
                window,
                kernel[down_step, side_step],
                preferred_element_type=jnp.float32,
            )
    return summed


def moments(values, positions):
    first_sum = jnp.sum(values, axis=(1, 2))
    second_sum = jnp.sum(values * values, axis=(1, 2))
    first_sum, second_sum = lax.psum((first_sum, second_sum), ("tr", "tc"))
    centre = first_sum / positions
    spread = second_sum / positions - centre * centre
    return (centre, lax.rsqrt(spread + 1e-05))


def normalize(values, centre, inverse):
    return jax.nn.relu((values - centre[:, None, None, :]) * inverse[:, None, None, :])


def widen(values):
    return with_halo(values, (("tr", 1), ("tc", 2)), 1)


def encode(frames, first_kernel, second_kernel, out_proj, out_bias):
    tile_rows = frames.shape[1]
    tile_cols = frames.shape[2]
    row_tiles = lax.axis_size("tr")
    col_tiles = lax.axis_size("tc")
    positions = float(tile_rows * row_tiles * tile_cols * col_tiles)
    first = convolve(widen(frames), first_kernel)
    centre, inverse = moments(first, positions)
    hidden = normalize(first, centre, inverse).astype(jnp.bfloat16)
    second = convolve(widen(hidden), second_kernel)
    centre, inverse = moments(second, positions)
    blocks = jax.nn.relu(frames.astype(jnp.float32) + normalize(second, centre, inverse)).astype(
        jnp.bfloat16
    )
    projected = (
        jnp.einsum("fhwc,cd->fhwd", blocks, out_proj, preferred_element_type=jnp.float32) + out_bias
    )
    return projected.astype(jnp.bfloat16)


def pool_block(blocks, factor):
    queries, pieces, height, across = blocks.shape
    if factor <= height:
        shaped = blocks.reshape(queries, pieces, height // factor, factor, across // factor, factor)
    else:
        shaped = blocks.reshape(queries, pieces, 1, height, across // factor, factor)
    return jnp.sum(shaped, axis=(3, 5))


def place(slots, matches, first_slot, base_level):
    updated = []
    for level_index, slot in zip((1, 2, 3), slots):
        factor = 2 ** (level_index - base_level)
        pooled = pool_block(matches, factor) / float(factor * factor)
        updated.append(
            lax.dynamic_update_slice_in_dim(slot, pooled.astype(slot.dtype), first_slot, 1)
        )
    return tuple(updated)


def settle(slots, level_index, tile_rows, row_tiles, col_tiles):
    queries = slots.shape[0]
    kept_rows = slots.shape[2]
    across = slots.shape[3]
    layout = slots.reshape(queries, row_tiles, col_tiles, kept_rows, across)
    factor = 2**level_index
    if factor <= tile_rows:
        layout = jnp.transpose(layout, (0, 1, 3, 2, 4))
    else:
        grouped = factor // tile_rows
        layout = jnp.sum(
            layout.reshape(queries, row_tiles // grouped, grouped, col_tiles, kept_rows, across),
            axis=2,
        )
    return layout.reshape(queries, -1).astype(jnp.bfloat16)


def body(frame_one, frame_two, first_kernel, second_kernel, out_proj, out_bias):
    frames = jnp.stack([frame_one, frame_two])
    feature = encode(frames, first_kernel, second_kernel, out_proj, out_bias)
    tile_rows = frame_one.shape[0]
    tile_cols = frame_one.shape[1]
    channels = feature.shape[3]
    row_tiles = lax.axis_size("tr")
    col_tiles = lax.axis_size("tc")
    devices = row_tiles * col_tiles
    inv_root = 1.0 / math.sqrt(channels)
    queries = feature[0].reshape(tile_rows * tile_cols, channels)
    query_count = tile_rows * tile_cols
    initial = []
    for level_index in (1, 2, 3):
        factor = 2**level_index
        kept_rows = max(tile_rows // factor, 1)
        slot_type = jnp.bfloat16 if factor <= tile_rows else jnp.float32
        initial.append(jnp.zeros((query_count, devices, kept_rows, tile_cols // factor), slot_type))
    initial = tuple(initial)

    def product(subset):
        return jnp.einsum("qc,gkc->qgk", queries, subset, preferred_element_type=jnp.float32)

    averaged = (
        jnp.sum(
            feature[1].astype(jnp.float32).reshape(tile_rows // 2, 2, tile_cols // 2, 2, channels),
            axis=(1, 3),
        )
        * 0.25
    )
    panel_rows = tile_rows // 2
    panel_cols = tile_cols // 2
    panel = (
        (lax.all_gather(averaged[None].astype(jnp.bfloat16), ("tr", "tc"), axis=0, tiled=True),)[
            0
        ].astype(jnp.float32),
    )
    pieces = panel[0].shape[0]
    group_size = math.gcd(pieces, 16)

    def advance(turn_index, carried):
        offset = turn_index * group_size
        matches = jnp.zeros((query_count, group_size, panel_rows * panel_cols), jnp.float32)
        for member in panel:
            subset = lax.dynamic_slice_in_dim(member, offset, group_size, 0)
            subset = subset.reshape(group_size, panel_rows * panel_cols, channels)
            if subset.dtype == jnp.float32:
                leading = subset.astype(jnp.bfloat16)
                trailing = (subset - leading.astype(jnp.float32)).astype(jnp.bfloat16)
                matches = product(leading) + product(trailing)
            else:
                matches = product(subset)
        matches = (matches * inv_root).reshape(query_count, group_size, panel_rows, panel_cols)
        return place(carried, matches, offset, 1)

    slots = lax.fori_loop(0, pieces // group_size, advance, initial)
    results = []
    for level_index, slot in zip((1, 2, 3), slots):
        results.append(
            settle(slot, level_index, tile_rows, row_tiles, col_tiles).reshape(
                tile_rows, tile_cols, -1
            )
        )
    return (results[0], results[1], results[2])


def solution(mesh):
    in_specs = (P("tr", "tc", None), P("tr", "tc", None), P(), P(), P(), P())
    out_specs = (P("tr", "tc", None), P("tr", "tc", None), P("tr", "tc", None))
    return jax.shard_map(body, mesh=mesh, in_specs=in_specs, out_specs=out_specs, check_vma=False)
```

profile of v0, /device:TPU:0, one launch (start us, length us, event | category | flops | bytes accessed | tf_op | source)
XLA Modules:
  0.0 168.6 jit_solution(14430870355920624105)
XLA Ops:
  0.7 0.8 fusion.68
  1.5 4.8 %collective-permute-start = (bf16[2,1,64,128]{3,2,1,0:T(8,128)(2,1)S(1)}, bf16[2,1,64,128]{3,2,1,0:T(8,128)(2,1)S(1)}, u32[]{:S(2)}, u32[]{:S(2)}) collective-permute-start(bf16[2,1,64,128]{3,2,1,0:T(8,128)(2,1)S(1)} %get-tuple-element.158), channel_id=1, source_target_pairs={{0,4},{4,8},{8,12},{12,16},{16,20},{20,24},{24,28},{1,5},{5,9},{9,... | collective-permute-start | bytes 98312 | tf_op jit(solution)/shard_map/ppermute | solution.py:14
  6.3 1.3 collective-permute-start.1
  7.7 0.9 fusion.67
  8.6 3.6 %collective-permute-done.1 = bf16[2,1,64,128]{3,2,1,0:T(8,128)(2,1)S(1)} collective-permute-done((bf16[2,1,64,128]{3,2,1,0:T(8,128)(2,1)S(1)}, bf16[2,1,64,128]{3,2,1,0:T(8,128)(2,1)S(1)}, u32[]{:S(2)}, u32[]{:S(2)}) %collective-permute-start.1) | collective-permute-done | bytes 32800 | tf_op jit(solution)/shard_map/ppermute | solution.py:17
  12.2 1.3 collective-permute-start.2
  13.5 1.3 collective-permute-start.3
  15.1 3.2 %collective-permute-done.3 = bf16[2,4,1,128]{3,2,1,0:T(2,128)(2,1)S(1)} collective-permute-done((bf16[2,4,1,128]{3,2,1,0:T(2,128)(2,1)S(1)}, bf16[2,4,1,128]{3,2,1,0:T(2,128)(2,1)S(1)}, u32[]{:S(2)}, u32[]{:S(2)}) %collective-permute-start.3) | collective-permute-done | bytes 2080 | tf_op jit(solution)/shard_map/ppermute | solution.py:17
  19.3 42.3 %all-reduce.1 = (f32[2,128]{1,0:T(2,128)S(1)}, f32[2,128]{1,0:T(2,128)S(1)}) all-reduce(f32[2,128]{1,0:T(2,128)S(1)} %get-tuple-element.129, f32[2,128]{1,0:T(2,128)S(1)} %get-tuple-element.128), channel_id=1, replica_groups=mesh['tr'=8,'tc'=4] {'tr','tc'}, use_global_device_ids=true, to_apply=%region_3.0 | all-reduce | flops 512 | bytes 4096 | tf_op jit(solution)/shard_map/psum | solution.py:43
  61.7 4.2 %collective-permute-start.4 = (bf16[2,1,64,128]{3,2,1,0:T(8,128)(2,1)S(1)}, bf16[2,1,64,128]{3,2,1,0:T(8,128)(2,1)S(1)}, u32[]{:S(2)}, u32[]{:S(2)}) collective-permute-start(bf16[2,1,64,128]{3,2,1,0:T(8,128)(2,1)S(1)} %get-tuple-element.156), channel_id=1, source_target_pairs={{0,4},{4,8},{8,12},{12,16},{16,20},{20,24},{24,28},{1,5},{5,9},{9,... | collective-permute-start | bytes 98312 | tf_op jit(solution)/shard_map/ppermute | solution.py:14
  65.9 1.3 collective-permute-start.5
  67.3 0.3 collective-permute-done.4
  67.7 4.0 %collective-permute-done.5 = bf16[2,1,64,128]{3,2,1,0:T(8,128)(2,1)S(1)} collective-permute-done((bf16[2,1,64,128]{3,2,1,0:T(8,128)(2,1)S(1)}, bf16[2,1,64,128]{3,2,1,0:T(8,128)(2,1)S(1)}, u32[]{:S(2)}, u32[]{:S(2)}) %collective-permute-start.5) | collective-permute-done | bytes 32800 | tf_op jit(solution)/shard_map/ppermute | solution.py:17
  71.7 1.3 collective-permute-start.6
  73.0 1.3 collective-permute-start.7
  74.6 1.7 %collective-permute-done.7 = bf16[2,4,1,128]{3,2,1,0:T(2,128)(2,1)S(1)} collective-permute-done((bf16[2,4,1,128]{3,2,1,0:T(2,128)(2,1)S(1)}, bf16[2,4,1,128]{3,2,1,0:T(2,128)(2,1)S(1)}, u32[]{:S(2)}, u32[]{:S(2)}) %collective-permute-start.7) | collective-permute-done | bytes 2080 | tf_op jit(solution)/shard_map/ppermute | solution.py:17
  77.3 42.4 %all-reduce = (f32[2,128]{1,0:T(2,128)S(1)}, f32[2,128]{1,0:T(2,128)S(1)}) all-reduce(f32[2,128]{1,0:T(2,128)S(1)} %get-tuple-element.127, f32[2,128]{1,0:T(2,128)S(1)} %get-tuple-element.126), channel_id=1, replica_groups=mesh['tr'=8,'tc'=4] {'tr','tc'}, use_global_device_ids=true, to_apply=%region_7.8 | all-reduce | flops 512 | bytes 4096 | tf_op jit(solution)/shard_map/psum | solution.py:43
  119.8 0.7 copy-done.6
  120.6 0.6 copy-done.1
  121.4 41.2 %all-gather = bf16[1024,256]{1,0:T(8,128)(2,1)S(1)} all-gather(bf16[32,256]{1,0:T(8,128)(2,1)S(1)} %multiply_convert_fusion), channel_id=2, replica_groups=mesh['tr'=8,'tc'=4] {'tr','tc'}, dimensions={0}, use_global_device_ids=true | all-gather | bytes 540672 | tf_op jit(solution)/shard_map/all_gather | solution.py:147
  162.8 0.8 slice-done
  163.6 2.1 %while.17 = (s32[]{:T(128)}, bf16[128,32,1,32]{0,3,1,2:T(8,128)(2,1)S(1)}, f32[128,32,1,16]{0,3,2,1:T(8,128)S(1)}, f32[128,32,1,8]{0,3,2,1:T(8,128)S(1)}, f32[32...) while((s32[]{:T(128)}, ...), condition=%wide.region_13.14_spmd, body=%wide.region_10.13_spmd.sunk | while | flops 67960832 | bytes 2950319 | solution.py:169
  163.6 0.2 fusion.122
  163.8 0.3 fusion.123
  164.3 0.3 reduce_sum.114
  164.6 0.2 fusion.122
  164.9 0.3 fusion.123
  165.3 0.3 reduce_sum.114
  165.8 0.7 copy.19
  166.6 0.7 copy.18
  167.3 0.2 reshape_reshape_transpose_reshape.3
  167.6 1.0 copy.17
  (60 shorter events, 3.8 us)
Async XLA Ops:
  0.6 119.1 %copy-start = (bf16[128,256]{1,0:T(8,128)(2,1)S(1)}, bf16[128,256]{1,0:T(8,128)(2,1)}, u32[]{:S(2)}) copy-start(bf16[128,256]{1,0:T(8,128)(2,1)} %param.12) | copy-start | bytes 196612
  0.6 7.0 %copy-start.2 = (bf16[2,64,128]{2,1,0:T(8,128)(2,1)S(1)}, bf16[2,64,128]{2,1,0:T(8,128)(2,1)}, u32[]{:S(2)}) copy-start(bf16[2,64,128]{2,1,0:T(8,128)(2,1)} %param.8) | copy-start | bytes 98308
  0.7 7.0 %copy-start.3 = (bf16[2,64,128]{2,1,0:T(8,128)(2,1)S(1)}, bf16[2,64,128]{2,1,0:T(8,128)(2,1)}, u32[]{:S(2)}) copy-start(bf16[2,64,128]{2,1,0:T(8,128)(2,1)} %param.9) | copy-start | bytes 98308
  0.7 14.1 %copy-start.5 = (bf16[3,3,128,128]{3,2,1,0:T(8,128)(2,1)S(1)}, bf16[3,3,128,128]{3,2,1,0:T(8,128)(2,1)}, u32[]{:S(2)}) copy-start(bf16[3,3,128,128]{3,2,1,0:T(8,128)(2,1)} %param.10) | copy-start | bytes 884740
  1.5 7.1 %collective-permute-start = (bf16[2,1,64,128]{3,2,1,0:T(8,128)(2,1)S(1)}, bf16[2,1,64,128]{3,2,1,0:T(8,128)(2,1)S(1)}, u32[]{:S(2)}, u32[]{:S(2)}) collective-permute-start(bf16[2,1,64,128]{3,2,1,0:T(8,128)(2,1)S(1)} %get-tuple-element.158), channel_id=1, source_target_pairs={{0,4},{4,8},{8,12},{12,16},{16,20},{20,24},{24,28},{1,5},{5,9},{9,... | collective-permute-start | bytes 98312 | tf_op jit(solution)/shard_map/ppermute | solution.py:14
  6.3 5.8 %collective-permute-start.1 = (bf16[2,1,64,128]{3,2,1,0:T(8,128)(2,1)S(1)}, bf16[2,1,64,128]{3,2,1,0:T(8,128)(2,1)S(1)}, u32[]{:S(2)}, u32[]{:S(2)}) collective-permute-start(bf16[2,1,64,128]{3,2,1,0:T(8,128)(2,1)S(1)} %get-tuple-element.159), channel_id=1, source_target_pairs={{4,0},{8,4},{12,8},{16,12},{20,16},{24,20},{28,24},{5,1},{9,5},{13... | collective-permute-start | bytes 98312 | tf_op jit(solution)/shard_map/ppermute | solution.py:17
  12.2 2.9 %collective-permute-start.2 = (bf16[2,4,1,128]{3,2,1,0:T(2,128)(2,1)S(1)}, bf16[2,4,1,128]{3,2,1,0:T(2,128)(2,1)S(1)}, u32[]{:S(2)}, u32[]{:S(2)}) collective-permute-start(bf16[2,4,1,128]{3,2,1,0:T(2,128)(2,1)S(1)} %get-tuple-element.154), channel_id=1, source_target_pairs={{0,1},{1,2},{2,3},{4,5},{5,6},{6,7},{8,9},{9,10},{10,11},{12,13},{... | collective-permute-start | bytes 6152 | tf_op jit(solution)/shard_map/ppermute | solution.py:14
  13.5 4.8 %collective-permute-start.3 = (bf16[2,4,1,128]{3,2,1,0:T(2,128)(2,1)S(1)}, bf16[2,4,1,128]{3,2,1,0:T(2,128)(2,1)S(1)}, u32[]{:S(2)}, u32[]{:S(2)}) collective-permute-start(bf16[2,4,1,128]{3,2,1,0:T(2,128)(2,1)S(1)} %get-tuple-element.155), channel_id=1, source_target_pairs={{1,0},{2,1},{3,2},{5,4},{6,5},{7,6},{9,8},{10,9},{11,10},{13,12},{... | collective-permute-start | bytes 6152 | tf_op jit(solution)/shard_map/ppermute | solution.py:17
  19.3 47.9 %copy-start.4 = (bf16[3,3,128,128]{3,2,1,0:T(8,128)(2,1)S(1)}, bf16[3,3,128,128]{3,2,1,0:T(8,128)(2,1)}, u32[]{:S(2)}) copy-start(bf16[3,3,128,128]{3,2,1,0:T(8,128)(2,1)} %param.11) | copy-start | bytes 884740
  61.7 6.0 %collective-permute-start.4 = (bf16[2,1,64,128]{3,2,1,0:T(8,128)(2,1)S(1)}, bf16[2,1,64,128]{3,2,1,0:T(8,128)(2,1)S(1)}, u32[]{:S(2)}, u32[]{:S(2)}) collective-permute-start(bf16[2,1,64,128]{3,2,1,0:T(8,128)(2,1)S(1)} %get-tuple-element.156), channel_id=1, source_target_pairs={{0,4},{4,8},{8,12},{12,16},{16,20},{20,24},{24,28},{1,5},{5,9},{9,... | collective-permute-start | bytes 98312 | tf_op jit(solution)/shard_map/ppermute | solution.py:14
  65.9 5.8 %collective-permute-start.5 = (bf16[2,1,64,128]{3,2,1,0:T(8,128)(2,1)S(1)}, bf16[2,1,64,128]{3,2,1,0:T(8,128)(2,1)S(1)}, u32[]{:S(2)}, u32[]{:S(2)}) collective-permute-start(bf16[2,1,64,128]{3,2,1,0:T(8,128)(2,1)S(1)} %get-tuple-element.157), channel_id=1, source_target_pairs={{4,0},{8,4},{12,8},{16,12},{20,16},{24,20},{28,24},{5,1},{9,5},{13... | collective-permute-start | bytes 98312 | tf_op jit(solution)/shard_map/ppermute | solution.py:17
  71.7 2.9 %collective-permute-start.6 = (bf16[2,4,1,128]{3,2,1,0:T(2,128)(2,1)S(1)}, bf16[2,4,1,128]{3,2,1,0:T(2,128)(2,1)S(1)}, u32[]{:S(2)}, u32[]{:S(2)}) collective-permute-start(bf16[2,4,1,128]{3,2,1,0:T(2,128)(2,1)S(1)} %get-tuple-element.150), channel_id=1, source_target_pairs={{0,1},{1,2},{2,3},{4,5},{5,6},{6,7},{8,9},{9,10},{10,11},{12,13},{... | collective-permute-start | bytes 6152 | tf_op jit(solution)/shard_map/ppermute | solution.py:14
  73.0 3.3 %collective-permute-start.7 = (bf16[2,4,1,128]{3,2,1,0:T(2,128)(2,1)S(1)}, bf16[2,4,1,128]{3,2,1,0:T(2,128)(2,1)S(1)}, u32[]{:S(2)}, u32[]{:S(2)}) collective-permute-start(bf16[2,4,1,128]{3,2,1,0:T(2,128)(2,1)S(1)} %get-tuple-element.151), channel_id=1, source_target_pairs={{1,0},{2,1},{3,2},{5,4},{6,5},{7,6},{9,8},{10,9},{11,10},{13,12},{... | collective-permute-start | bytes 6152 | tf_op jit(solution)/shard_map/ppermute | solution.py:17
  119.7 0.7 copy-start.6
  120.6 0.7 copy-start.1
  162.8 0.8 slice-start
where the time goes:
time: 169 us
  blocking collectives  126 us (75%)
  starting transfers between devices  16.8 us (10%)
  waiting for transfers between devices  12.8 us (8%)
  local copies, waits for them, and re-layouts  5.16 us (3%)
  matrix products  4.54 us (3%)
  other arithmetic  2.22 us (1%)
    psum x2, blocking collectives, moments(): first_sum, second_sum = lax.psum((first_sum, second_sum), ('tr', 'tc'))  84.7 us
    all_gather x1, blocking collectives, body(): lax.all_gather(averaged[None].astype(jnp.bfloat16), ('tr', 'tc'), axis=0,...  41.2 us
    ppermute x4, waiting for transfers between devices, with_halo(): lax.ppermute(lax.slice_in_dim(block, 0, width, axis=dim), axis, backward)  12.5 us
    ppermute x4, starting transfers between devices, with_halo(): lax.ppermute(lax.slice_in_dim(block, block.shape[dim] - width, None, axis...  11.6 us
    ppermute x4, starting transfers between devices, with_halo(): lax.ppermute(lax.slice_in_dim(block, 0, width, axis=dim), axis, backward)  5.17 us
    unnamed x17, local copies, waits for them, and re-layouts  3.82 us
    dot_general x18, matrix products, convolve(): jnp.einsum('fhwc,cd->fhwd', window, kernel[down_step, side_step], preferr...  3.42 us
  transfers between devices with their start and end apart: 8, of which 5 were waited for; matrix products, arithmetic and copies ran while one was open for 1% of the time, Pallas kernels for 0%

commit v1 on v0

v1 whole, which is shorter than its diff:
```python
import functools
import math

import jax
import jax.numpy as jnp
from jax import lax
from jax.experimental import pallas as pl
from jax.experimental.pallas import tpu as pltpu
from jax.sharding import PartitionSpec as P

MESH = pl.DeviceIdType.MESH
F32 = jnp.float32
BF16 = jnp.bfloat16


def dot_t(a, b):
    return lax.dot_general(a, b, (((1,), (1,)), ((), ())), preferred_element_type=F32)


def split(values):
    high = values.astype(BF16)
    low = (values - high.astype(F32)).astype(BF16)
    return high, low


def kernel(
    row_tiles, col_tiles, rows, cols,
    f1, f2, w1_hbm, w2_hbm, wp_hbm, bias_hbm,
    o1, o2, o3,
    w1, w2, wp, bias,
    tiles, edge_rows, edge_out, edge_in,
    grid, patches, conv_own, conv_edge, hidden, patches2,
    stat_one, stat_two, keys, pool_a, pool_b, pool_c,
    in_sem, row_send, row_recv, edge_send, edge_recv, all_send, all_recv,
):
    tr = lax.axis_index("tr")
    tc = lax.axis_index("tc")
    devices = row_tiles * col_tiles
    me = tr * col_tiles + tc
    positions = float(devices * rows * cols)
    channels = wp.shape[1]
    pooled_cols = cols // 2

    loads = [
        pltpu.make_async_copy(f1, tiles.at[0], in_sem.at[0]),
        pltpu.make_async_copy(f2, tiles.at[1], in_sem.at[1]),
        pltpu.make_async_copy(w1_hbm, w1, in_sem.at[2]),
        pltpu.make_async_copy(w2_hbm, w2, in_sem.at[3]),
        pltpu.make_async_copy(wp_hbm, wp, in_sem.at[4]),
        pltpu.make_async_copy(bias_hbm, bias, in_sem.at[5]),
    ]
    for load in loads:
        load.start()

    edge_rows[...] = jnp.zeros_like(edge_rows)
    edge_in[...] = jnp.zeros_like(edge_in)

    def place_of(index):
        return (index // col_tiles, lax.rem(index, col_tiles))

    barrier = pltpu.get_barrier_semaphore()

    def greet(step, carried):
        other = lax.rem(me + step, devices)
        pl.semaphore_signal(barrier, inc=1, device_id=place_of(other), device_id_type=MESH)
        return carried

    lax.fori_loop(1, devices, greet, 0)

    loads[0].wait()
    loads[1].wait()
    left = 16
    right = left + cols
    for f in range(2):
        for y in range(2):
            values = tiles[f, y].astype(F32)
            grid[f, 2 + y, left:right, :] = values
            line = f * 4 + y * 2
            edge_out[0, line:line + 2, :] = values[0:2]
            edge_out[1, line:line + 2, :] = values[cols - 2:cols]

    pl.semaphore_wait(barrier, devices - 1)

    def inside(down, side):
        row = tr + down
        col = tc + side
        return (row >= 0) & (row < row_tiles) & (col >= 0) & (col < col_tiles)

    corners = [
        (0, 1, 1, 0), (0, -1, 0, 1),
        (1, 1, 1, 2), (1, -1, 0, 3),
        (-1, 1, 1, 4), (-1, -1, 0, 5),
    ]
    lines = [(1, 1, 0), (-1, 0, 1), (1, 0, 2), (-1, 1, 3)]

    def row_copies(down, row, slot):
        return [
            pltpu.make_async_remote_copy(
                src_ref=frame.at[row], dst_ref=edge_rows.at[slot, f],
                send_sem=row_send.at[slot], recv_sem=row_recv.at[slot],
                device_id=(tr + down, tc), device_id_type=MESH,
            )
            for f, frame in enumerate((f1, f2))
        ]

    def edge_copy(down, side, which, slot):
        return pltpu.make_async_remote_copy(
            src_ref=edge_out.at[which], dst_ref=edge_in.at[slot],
            send_sem=edge_send.at[slot], recv_sem=edge_recv.at[slot],
            device_id=(tr + down, tc + side), device_id_type=MESH,
        )

    def send_row(line):
        @pl.when(inside(line[0], 0))
        def _():
            for copy in row_copies(*line):
                copy.start()

    def send_edge(corner):
        @pl.when(inside(corner[0], corner[1]))
        def _():
            edge_copy(*corner).start()

    def await_row(line):
        slot = line[2]

        @pl.when(inside(-line[0], 0))
        def _():
            pltpu.make_async_copy(edge_rows.at[slot], edge_rows.at[slot], row_recv.at[slot]).wait()

    def await_edge(corner):
        slot = corner[3]

        @pl.when(inside(-corner[0], -corner[1]))
        def _():
            pltpu.make_async_copy(edge_in.at[slot], edge_in.at[slot], edge_recv.at[slot]).wait()

    for line in lines[:2]:
        send_row(line)
    for corner in corners:
        send_edge(corner)
    for line in lines[2:]:
        send_row(line)

    def fill_row(y, slot):
        for f in range(2):
            grid[f, y, left:right, :] = edge_rows[slot, f].astype(F32)

    def fill_edges(y, slot, base):
        for f in range(2):
            line = f * 4 + base * 2
            grid[f, y, left - 2:left, :] = edge_in[slot, line:line + 2, :]
            grid[f, y, right:right + 2, :] = edge_in[slot + 1, line:line + 2, :]

    wide = cols + 16

    def fill_patches(y):
        for f in range(2):
            for j in range(3):
                start = left - 9 + j
                patches[f, y, :, j * 128:(j + 1) * 128] = grid[f, y, start:start + wide, :].astype(BF16)

    for line in lines[:2]:
        await_row(line)
    for corner in corners:
        await_edge(corner)
    fill_row(1, 0)
    fill_row(4, 1)
    for y in range(2):
        fill_edges(2 + y, 0, y)
        fill_edges(0 + y, 2, y)
        fill_edges(4 + y, 4, y)
    for y in range(1, 5):
        fill_patches(y)

    loads[2].wait()

    def convolve(first_row, count):
        total = None
        for i in range(3):
            window = patches[:, first_row - 1 + i:first_row - 1 + i + count]
            part = jnp.dot(window.reshape(2 * count * wide, 384), w1[i], preferred_element_type=F32)
            total = part if total is None else total + part
        return total.reshape(2, count, wide, 128)

    def share(stats, slots, phase):
        slots[me] = stats

        def give(step, carried):
            other = lax.rem(me + step, devices)
            pltpu.make_async_remote_copy(
                src_ref=slots.at[me], dst_ref=slots.at[me],
                send_sem=all_send.at[phase], recv_sem=all_recv.at[phase],
                device_id=place_of(other), device_id_type=MESH,
            ).start()
            return carried

        lax.fori_loop(1, devices, give, 0)

    def sums_of(values):
        total = jnp.sum(values, axis=(1, 2))
        squares = jnp.sum(values * values, axis=(1, 2))
        return jnp.concatenate([total, squares], axis=0)

    def collect(slots, phase):
        others = slots.at[pl.ds(0, devices - 1)]
        pltpu.make_async_copy(others, others, all_recv.at[phase]).wait()
        total = jnp.sum(slots[...], axis=0) / positions
        centre = total[0:2]
        spread = total[2:4] - centre * centre
        return centre[:, None, None, :], lax.rsqrt(spread + 1e-05)[:, None, None, :]

    own = convolve(2, 2)
    conv_own[...] = own
    share(sums_of(own[:, :, 8:8 + cols]), stat_one, 0)

    for line in lines[2:]:
        await_row(line)
    fill_row(0, 2)
    fill_row(5, 3)
    fill_patches(0)
    fill_patches(5)
    conv_edge[:, 0:1] = convolve(1, 1)
    conv_edge[:, 1:2] = convolve(4, 1)
    loads[3].wait()

    centre, inverse = collect(stat_one, 0)
    spot = lax.broadcasted_iota(jnp.int32, (1, 1, wide, 128), 2)
    col_ok = ((spot >= 8) | (tc > 0)) & ((spot < 8 + cols) | (tc < col_tiles - 1))

    def normal(values, keep):
        return jnp.where(keep, jax.nn.relu((values - centre) * inverse), 0.0)

    hidden[:, 1:3, 8:8 + wide, :] = normal(conv_own[...], col_ok)
    hidden[:, 0:1, 8:8 + wide, :] = normal(conv_edge[:, 0:1], col_ok & (tr > 0))
    hidden[:, 3:4, 8:8 + wide, :] = normal(conv_edge[:, 1:2], col_ok & (tr < row_tiles - 1))
    for f in range(2):
        for y in range(4):
            for j in range(3):
                start = left - 1 + j
                patches2[f, y, :, j * 128:(j + 1) * 128] = hidden[f, y, start:start + cols, :].astype(BF16)
    second = None
    for i in range(3):
        window = patches2[:, i:i + 2].reshape(4 * cols, 384)
        part = jnp.dot(window, w2[i], preferred_element_type=F32)
        second = part if second is None else second + part
    second = second.reshape(2, 2, cols, 128)
    share(sums_of(second), stat_two, 1)
    loads[4].wait()
    loads[5].wait()
    centre, inverse = collect(stat_two, 1)
    blocks = jax.nn.relu(tiles[...].astype(F32) + jax.nn.relu((second - centre) * inverse)).astype(BF16)

    pool_a[0:cols, :] = blocks[1, 0].astype(F32) + blocks[1, 1].astype(F32)
    small = (pool_a[pl.ds(0, pooled_cols, stride=2), :] + pool_a[pl.ds(1, pooled_cols, stride=2), :]) * 0.25
    mine = pl.ds(pl.multiple_of(me * pooled_cols, pooled_cols), pooled_cols)
    keys[mine, :] = small.astype(BF16)

    def give_keys(step, carried):
        other = lax.rem(me + step, devices)
        pltpu.make_async_remote_copy(
            src_ref=keys.at[mine], dst_ref=keys.at[mine],
            send_sem=all_send.at[2], recv_sem=all_recv.at[2],
            device_id=place_of(other), device_id_type=MESH,
        ).start()
        return carried

    lax.fori_loop(1, devices, give_keys, 0)

    scale = 1.0 / math.sqrt(channels)
    feature = jnp.dot(blocks[0].reshape(2 * cols, 128), wp[...], preferred_element_type=F32) + bias[...]
    feature = feature.astype(BF16)
    offset = jnp.sum(feature.astype(F32) * bias[...], axis=1, keepdims=True) * scale
    high, low = split(dot_t(feature, wp[...]) * scale)
    queries = jnp.concatenate([high, low], axis=1)

    others = keys.at[pl.ds(0, (devices - 1) * pooled_cols)]
    pltpu.make_async_copy(others, others, all_recv.at[2]).wait()

    across = col_tiles * pooled_cols
    total_keys = devices * pooled_cols
    chunk = min(total_keys, 2048)
    lines1 = chunk // across

    def pooled(values, scratch, lines_in, width):
        pairs = jnp.sum(values.reshape(lines_in // 2, 2, width, 128), axis=1)
        count = lines_in // 2 * width
        scratch[0:count, :] = pairs.reshape(count, 128)
        half = count // 2
        return (scratch[pl.ds(0, half, stride=2), :] + scratch[pl.ds(1, half, stride=2), :]) * 0.25

    def fine(values):
        k_high, k_low = split(values)
        return dot_t(queries, jnp.concatenate([k_high, k_high], axis=1)) + dot_t(high, k_low) + offset

    for start in range(0, total_keys, chunk):
        part = keys[start:start + chunk, :]
        level = dot_t(queries, jnp.concatenate([part, part], axis=1)) + offset
        o1[:, start:start + chunk] = level.astype(BF16)
        two = pooled(part.astype(F32), pool_b, lines1, across)
        o2[:, start // 4:(start + chunk) // 4] = fine(two).astype(BF16)
        three = pooled(two, pool_c, lines1 // 2, across // 2)
        o3[:, start // 16:(start + chunk) // 16] = fine(three).astype(BF16)

    for line in lines:
        slot = line[2]

        @pl.when(inside(line[0], 0))
        def _(slot=slot):
            pltpu.make_async_copy(edge_rows.at[slot], edge_rows.at[slot], row_send.at[slot]).wait()

    for corner in corners:
        slot = corner[3]

        @pl.when(inside(corner[0], corner[1]))
        def _(slot=slot):
            pltpu.make_async_copy(edge_in.at[slot], edge_in.at[slot], edge_send.at[slot]).wait()

    for phase, slots in enumerate((stat_one, stat_two)):
        gone = slots.at[pl.ds(0, devices - 1)]
        pltpu.make_async_copy(gone, gone, all_send.at[phase]).wait()
    pltpu.make_async_copy(others, others, all_send.at[2]).wait()


def body(row_tiles, col_tiles, frame_one, frame_two, first_kernel, second_kernel, out_proj, out_bias):
    rows, cols, cin = frame_one.shape
    channels = out_proj.shape[1]
    devices = row_tiles * col_tiles
    queries = rows * cols
    keys = devices * queries // 4
    wide = cols + 16
    chunk = min(keys, 2048)
    vmem = pltpu.VMEM
    anywhere = pl.BlockSpec(memory_space=pl.ANY)
    local = pl.BlockSpec(memory_space=pltpu.VMEM)
    outs = pl.pallas_call(
        functools.partial(kernel, row_tiles, col_tiles, rows, cols),
        out_shape=[
            jax.ShapeDtypeStruct((queries, keys), BF16),
            jax.ShapeDtypeStruct((queries, keys // 4), BF16),
            jax.ShapeDtypeStruct((queries, keys // 16), BF16),
        ],
        in_specs=[anywhere] * 6,
        out_specs=[local] * 3,
        scratch_shapes=[
            vmem((3, 3 * cin, cin), BF16),
            vmem((3, 3 * cin, cin), BF16),
            vmem((cin, channels), BF16),
            vmem((1, channels), F32),
            vmem((2, rows, cols, cin), BF16),
            vmem((4, 2, cols, cin), BF16),
            vmem((2, 8, cin), F32),
            vmem((6, 8, cin), F32),
            vmem((2, 6, cols + 32, cin), F32),
            vmem((2, 6, wide, 3 * cin), BF16),
            vmem((2, 2, wide, cin), F32),
            vmem((2, 2, wide, cin), F32),
            vmem((2, 4, cols + 32, cin), F32),
            vmem((2, 4, cols, 3 * cin), BF16),
            vmem((devices, 4, cin), F32),
            vmem((devices, 4, cin), F32),
            vmem((keys, cin), BF16),
            vmem((cols, cin), F32),
            vmem((chunk // 2, cin), F32),
            vmem((chunk // 8, cin), F32),
            pltpu.SemaphoreType.DMA((6,)),
            pltpu.SemaphoreType.DMA((4,)),
            pltpu.SemaphoreType.DMA((4,)),
            pltpu.SemaphoreType.DMA((6,)),
            pltpu.SemaphoreType.DMA((6,)),
            pltpu.SemaphoreType.DMA((3,)),
            pltpu.SemaphoreType.DMA((3,)),
        ],
        compiler_params=pltpu.CompilerParams(
            collective_id=0, has_side_effects=True, vmem_limit_bytes=48 * 1024 * 1024
        ),
    )(
        frame_one, frame_two,
        first_kernel.reshape(3, 3 * cin, cin), second_kernel.reshape(3, 3 * cin, cin),
        out_proj, out_bias.reshape(1, channels),
    )
    return tuple(out.reshape(rows, cols, -1) for out in outs)


def solution(mesh):
    in_specs = (P("tr", "tc", None), P("tr", "tc", None), P(), P(), P(), P())
    out_specs = (P("tr", "tc", None), P("tr", "tc", None), P("tr", "tc", None))
    step = functools.partial(body, mesh.shape["tr"], mesh.shape["tc"])
    return jax.shard_map(step, mesh=mesh, in_specs=in_specs, out_specs=out_specs, check_vma=False)
```

time: 169 us -> 36.7 us (0.22)
  blocking collectives: 126 us -> 0 us
  Pallas kernels: 0 us -> 28.7 us
  starting transfers between devices: 16.8 us -> 0 us
  waiting for transfers between devices: 12.8 us -> 0 us
  matrix products: 4.54 us -> 0 us
  other arithmetic: 2.22 us -> 0 us
  local copies, waits for them, and re-layouts: 5.16 us -> 6.9 us
    psum x2 -> x0, blocking collectives: 84.7 us -> none  [moments(): first_sum, second_sum = lax.psum((first_sum, second_sum), ('tr', 'tc'))]
    all_gather x1 -> x0, blocking collectives: 41.2 us -> none  [body(): lax.all_gather(averaged[None].astype(jnp.bfloat16), ('tr', 'tc'), axis=0,...]
    pallas_call x0 -> x1, Pallas kernels: none -> 28.7 us  [body(): pl.pallas_call(functools.partial(kernel, row_tiles, col_tiles, rows, cols...]
    ppermute x8 -> x0, starting transfers between devices: 16.8 us -> none  [the longest x4 11.6 us: with_halo(): lax.ppermute(lax.slice_in_dim(block, block.shape[dim] - width, None, axis...]
    ppermute x8 -> x0, waiting for transfers between devices: 12.8 us -> none  [the longest x4 12.5 us: with_halo(): lax.ppermute(lax.slice_in_dim(block, 0, width, axis=dim), axis, backward)]
    dot_general x23 -> x0, matrix products: 4.54 us -> none  [the longest x18 3.42 us: convolve(): jnp.einsum('fhwc,cd->fhwd', window, kernel[down_step, side_step], preferr...]
    unnamed x17 -> x15, local copies, waits for them, and re-layouts: 3.82 us -> 6.9 us
  transfers between devices with their start and end apart: 8 -> 0, of which waited for: 5 -> 0; matrix products, arithmetic and copies ran while one was open for 1% -> 0% of each run, Pallas kernels for 0% -> 0%
where the time goes in v1:
time: 36.7 us; the launch traced here: 36.3 us
  Pallas kernels  28.7 us (78%)
  local copies, waits for them, and re-layouts  6.9 us (19%)
  between operations  0.65 us (2%)
    pallas_call x1, Pallas kernels, body(): pl.pallas_call(functools.partial(kernel, row_tiles, col_tiles, rows, cols...  28.7 us
    unnamed x15, local copies, waits for them, and re-layouts  6.9 us

profile of v1, /device:TPU:0, one launch (start us, length us, event | category | flops | bytes accessed | tf_op | source)
XLA Modules:
  0.0 36.3 jit_solution(5275260950218594614)
XLA Ops:
  0.6 0.0 copy-start.5
  0.6 0.7 %copy-done.5 = f32[256]{0:T(256)S(1)} copy-done((f32[256]{0:T(256)S(1)}, f32[256]{0:T(256)}, u32[]{:S(2)}) %copy-start.5) | copy-done | bytes 1048
  1.3 0.0 copy-start
  1.3 1.0 %copy-done = bf16[3,3,128,128]{3,2,1,0:T(8,128)(2,1)S(1)} copy-done((bf16[3,3,128,128]{3,2,1,0:T(8,128)(2,1)S(1)}, bf16[3,3,128,128]{3,2,1,0:T(8,128)(2,1)}, u32[]{:S(2)}) %copy-start) | copy-done | bytes 294936
  2.3 0.0 copy-start.1
  2.3 1.0 %copy-done.1 = bf16[3,3,128,128]{3,2,1,0:T(8,128)(2,1)S(1)} copy-done((bf16[3,3,128,128]{3,2,1,0:T(8,128)(2,1)S(1)}, bf16[3,3,128,128]{3,2,1,0:T(8,128)(2,1)}, u32[]{:S(2)}) %copy-start.1) | copy-done | bytes 294936
  3.2 0.0 copy-start.2
  3.2 0.8 %copy-done.2 = bf16[128,256]{1,0:T(8,128)(2,1)S(1)} copy-done((bf16[128,256]{1,0:T(8,128)(2,1)S(1)}, bf16[128,256]{1,0:T(8,128)(2,1)}, u32[]{:S(2)}) %copy-start.2) | copy-done | bytes 65560
  4.1 0.0 copy-start.3
  4.1 0.8 %copy-done.3 = bf16[2,64,128]{2,1,0:T(8,128)(2,1)S(1)} copy-done((bf16[2,64,128]{2,1,0:T(8,128)(2,1)S(1)}, bf16[2,64,128]{2,1,0:T(8,128)(2,1)}, u32[]{:S(2)}) %copy-start.3) | copy-done | bytes 32792
  4.8 0.0 copy-start.4
  4.8 0.8 %copy-done.4 = bf16[2,64,128]{2,1,0:T(8,128)(2,1)S(1)} copy-done((bf16[2,64,128]{2,1,0:T(8,128)(2,1)S(1)}, bf16[2,64,128]{2,1,0:T(8,128)(2,1)}, u32[]{:S(2)}) %copy-start.4) | copy-done | bytes 32792
  5.6 28.7 %shard_map.85 = (bf16[128,1024]{1,0:T(8,128)(2,1)S(1)}, bf16[128,256]{1,0:T(8,128)(2,1)S(1)}, bf16[128,64]{1,0:T(8,128)(2,1)S(1)}) custom-call(bf16[2,64,128]{2,1,0:T(8,128)(2,1)S(1)} %copy-done.3, bf16[2,64,128]{2,1,0:T(8,128)(2,1)S(1)} %copy-done.4, bf16[3,384,128]{2,1,0:T(8,128)(2,1)S(1)} %bitcast.6, bf16[3,384,128]{2,1,0:T(8,128)(2,1)S(1)} %bitcast.7, ...), custom_call_target="tpu_custom_call" | custom-call | tf_op jit(solution)/shard_map/pallas_call | solution.py:336
  34.3 0.7 %copy.12 = bf16[2,64,1024]{2,1,0:T(8,128)(2,1)} copy(bf16[2,64,1024]{2,1,0:T(8,128)(2,1)S(1)} %bitcast.8) | data formatting | bytes 524288
  35.0 0.6 %copy.13 = bf16[2,64,256]{2,1,0:T(8,128)(2,1)} copy(bf16[2,64,256]{2,1,0:T(8,128)(2,1)S(1)} %bitcast.9) | data formatting | bytes 131072
  35.7 0.6 %copy.14 = bf16[2,64,64]{2,1,0:T(8,128)(2,1)} copy(bf16[2,64,64]{2,1,0:T(8,128)(2,1)S(1)} %bitcast.10) | data formatting | bytes 32768
Async XLA Ops:
  0.6 0.7 %copy-start.5 = (f32[256]{0:T(256)S(1)}, f32[256]{0:T(256)}, u32[]{:S(2)}) copy-start(f32[256]{0:T(256)} %param.11) | copy-start | bytes 3076
  1.3 1.0 %copy-start = (bf16[3,3,128,128]{3,2,1,0:T(8,128)(2,1)S(1)}, bf16[3,3,128,128]{3,2,1,0:T(8,128)(2,1)}, u32[]{:S(2)}) copy-start(bf16[3,3,128,128]{3,2,1,0:T(8,128)(2,1)} %param.8) | copy-start | bytes 884740
  2.3 1.0 %copy-start.1 = (bf16[3,3,128,128]{3,2,1,0:T(8,128)(2,1)S(1)}, bf16[3,3,128,128]{3,2,1,0:T(8,128)(2,1)}, u32[]{:S(2)}) copy-start(bf16[3,3,128,128]{3,2,1,0:T(8,128)(2,1)} %param.9) | copy-start | bytes 884740
  3.2 0.8 %copy-start.2 = (bf16[128,256]{1,0:T(8,128)(2,1)S(1)}, bf16[128,256]{1,0:T(8,128)(2,1)}, u32[]{:S(2)}) copy-start(bf16[128,256]{1,0:T(8,128)(2,1)} %wp_hbm.1) | copy-start | bytes 196612
  4.1 0.8 %copy-start.3 = (bf16[2,64,128]{2,1,0:T(8,128)(2,1)S(1)}, bf16[2,64,128]{2,1,0:T(8,128)(2,1)}, u32[]{:S(2)}) copy-start(bf16[2,64,128]{2,1,0:T(8,128)(2,1)} %f1.1) | copy-start | bytes 98308
  4.8 0.8 %copy-start.4 = (bf16[2,64,128]{2,1,0:T(8,128)(2,1)S(1)}, bf16[2,64,128]{2,1,0:T(8,128)(2,1)}, u32[]{:S(2)}) copy-start(bf16[2,64,128]{2,1,0:T(8,128)(2,1)} %f2.1) | copy-start | bytes 98308

commit v2 on v1

--- a/solution.py
+++ b/solution.py
@@ -26,12 +26,12 @@
 def kernel(
     row_tiles, col_tiles, rows, cols,
     f1, f2, w1_hbm, w2_hbm, wp_hbm, bias_hbm,
-    o1, o2, o3,
+    keys, query_out, offset_out,
     w1, w2, wp, bias,
     tiles, edge_rows, edge_out, edge_in,
     grid, patches, conv_own, conv_edge, hidden, patches2,
-    stat_one, stat_two, keys, pool_a, pool_b, pool_c,
-    in_sem, row_send, row_recv, edge_send, edge_recv, all_send, all_recv,
+    near_one, far_one, near_two, far_two, pool_a,
+    in_sem, row_send, row_recv, edge_send, edge_recv, all_send, all_recv, line_recv,
 ):
     tr = lax.axis_index("tr")
     tc = lax.axis_index("tc")
@@ -55,17 +55,42 @@
     edge_rows[...] = jnp.zeros_like(edge_rows)
     edge_in[...] = jnp.zeros_like(edge_in)
 
-    def place_of(index):
-        return (index // col_tiles, lax.rem(index, col_tiles))
+    def inside(down, side):
+        row = tr + down
+        col = tc + side
+        return (row >= 0) & (row < row_tiles) & (col >= 0) & (col < col_tiles)
+
+    def along_rows(step):
+        return (lax.rem(tr + step, row_tiles), tc)
+
+    def along_cols(step):
+        return (tr, lax.rem(tc + step, col_tiles))
+
+    def each(count, act):
+        if count <= 8:
+            for step in sorted(range(1, count), key=lambda s: min(s, count - s)):
+                act(step)
+        else:
+            def turn(step, carried):
+                act(step)
+                return carried
+
+            lax.fori_loop(1, count, turn, 0)
 
     barrier = pltpu.get_barrier_semaphore()
 
-    def greet(step, carried):
-        other = lax.rem(me + step, devices)
-        pl.semaphore_signal(barrier, inc=1, device_id=place_of(other), device_id_type=MESH)
-        return carried
-
-    lax.fori_loop(1, devices, greet, 0)
+    def greet(place):
+        pl.semaphore_signal(barrier, inc=1, device_id=place, device_id_type=MESH)
+
+    each(row_tiles, lambda step: greet(along_rows(step)))
+    each(col_tiles, lambda step: greet(along_cols(step)))
+    greeted = row_tiles + col_tiles - 2
+    for down, side in ((1, 1), (1, -1), (-1, 1), (-1, -1)):
+        @pl.when(inside(down, side))
+        def _(down=down, side=side):
+            greet((tr + down, tc + side))
+
+        greeted = greeted + inside(down, side).astype(jnp.int32)
 
     loads[0].wait()
     loads[1].wait()
@@ -79,12 +104,7 @@
             edge_out[0, line:line + 2, :] = values[0:2]
             edge_out[1, line:line + 2, :] = values[cols - 2:cols]
 
-    pl.semaphore_wait(barrier, devices - 1)
-
-    def inside(down, side):
-        row = tr + down
-        col = tc + side
-        return (row >= 0) & (row < row_tiles) & (col >= 0) & (col < col_tiles)
+    pl.semaphore_wait(barrier, greeted)
 
     corners = [
         (0, 1, 1, 0), (0, -1, 0, 1),
@@ -183,36 +203,41 @@
             total = part if total is None else total + part
         return total.reshape(2, count, wide, 128)
 
+    def give(slots, mine, place, phase):
+        pltpu.make_async_remote_copy(
+            src_ref=slots.at[mine], dst_ref=slots.at[mine],
+            send_sem=all_send.at[phase], recv_sem=all_recv.at[phase],
+            device_id=place, device_id_type=MESH,
+        ).start()
+
+    def arrived(slots, count, sem):
+        others = slots.at[pl.ds(0, count)]
+        pltpu.make_async_copy(others, others, sem).wait()
+
     def share(stats, slots, phase):
-        slots[me] = stats
-
-        def give(step, carried):
-            other = lax.rem(me + step, devices)
-            pltpu.make_async_remote_copy(
-                src_ref=slots.at[me], dst_ref=slots.at[me],
-                send_sem=all_send.at[phase], recv_sem=all_recv.at[phase],
-                device_id=place_of(other), device_id_type=MESH,
-            ).start()
-            return carried
-
-        lax.fori_loop(1, devices, give, 0)
+        slots[tc] = stats
+        each(col_tiles, lambda step: give(slots, tc, along_cols(step), phase))
+
+    def pass_on(near, far, phase):
+        arrived(near, col_tiles - 1, all_recv.at[phase])
+        far[tr] = jnp.sum(near[...], axis=0)
+        each(row_tiles, lambda step: give(far, tr, along_rows(step), phase + 1))
 
     def sums_of(values):
         total = jnp.sum(values, axis=(1, 2))
         squares = jnp.sum(values * values, axis=(1, 2))
         return jnp.concatenate([total, squares], axis=0)
 
-    def collect(slots, phase):
-        others = slots.at[pl.ds(0, devices - 1)]
-        pltpu.make_async_copy(others, others, all_recv.at[phase]).wait()
-        total = jnp.sum(slots[...], axis=0) / positions
+    def collect(far, phase):
+        arrived(far, row_tiles - 1, all_recv.at[phase])
+        total = jnp.sum(far[...], axis=0) / positions
         centre = total[0:2]
         spread = total[2:4] - centre * centre
         return centre[:, None, None, :], lax.rsqrt(spread + 1e-05)[:, None, None, :]
 
     own = convolve(2, 2)
     conv_own[...] = own
-    share(sums_of(own[:, :, 8:8 + cols]), stat_one, 0)
+    share(sums_of(own[:, :, 8:8 + cols]), near_one, 0)
 
     for line in lines[2:]:
         await_row(line)
@@ -220,11 +245,12 @@
     fill_row(5, 3)
     fill_patches(0)
     fill_patches(5)
+    pass_on(near_one, far_one, 0)
     conv_edge[:, 0:1] = convolve(1, 1)
     conv_edge[:, 1:2] = convolve(4, 1)
     loads[3].wait()
 
-    centre, inverse = collect(stat_one, 0)
+    centre, inverse = collect(far_one, 1)
     spot = lax.broadcasted_iota(jnp.int32, (1, 1, wide, 128), 2)
     col_ok = ((spot >= 8) | (tc > 0)) & ((spot < 8 + cols) | (tc < col_tiles - 1))
 
@@ -245,27 +271,31 @@
         part = jnp.dot(window, w2[i], preferred_element_type=F32)
         second = part if second is None else second + part
     second = second.reshape(2, 2, cols, 128)
-    share(sums_of(second), stat_two, 1)
+    share(sums_of(second), near_two, 2)
     loads[4].wait()
     loads[5].wait()
-    centre, inverse = collect(stat_two, 1)
+    pass_on(near_two, far_two, 2)
+    centre, inverse = collect(far_two, 3)
     blocks = jax.nn.relu(tiles[...].astype(F32) + jax.nn.relu((second - centre) * inverse)).astype(BF16)
 
     pool_a[0:cols, :] = blocks[1, 0].astype(F32) + blocks[1, 1].astype(F32)
     small = (pool_a[pl.ds(0, pooled_cols, stride=2), :] + pool_a[pl.ds(1, pooled_cols, stride=2), :]) * 0.25
-    mine = pl.ds(pl.multiple_of(me * pooled_cols, pooled_cols), pooled_cols)
-    keys[mine, :] = small.astype(BF16)
-
-    def give_keys(step, carried):
-        other = lax.rem(me + step, devices)
-        pltpu.make_async_remote_copy(
-            src_ref=keys.at[mine], dst_ref=keys.at[mine],
-            send_sem=all_send.at[2], recv_sem=all_recv.at[2],
-            device_id=place_of(other), device_id_type=MESH,
-        ).start()
-        return carried
-
-    lax.fori_loop(1, devices, give_keys, 0)
+    keys[tr, tc] = small.astype(BF16)
+
+    def key_copy(row, place, send_sem, recv_sem):
+        return pltpu.make_async_remote_copy(
+            src_ref=keys.at[row, tc], dst_ref=keys.at[row, tc],
+            send_sem=send_sem, recv_sem=recv_sem,
+            device_id=place, device_id_type=MESH,
+        )
+
+    def spread_line(row):
+        each(col_tiles, lambda step: key_copy(
+            row, along_cols(step), all_send.at[5], all_recv.at[4]).start())
+
+    each(row_tiles, lambda step: key_copy(
+        tr, along_rows(step), all_send.at[4], line_recv.at[tr]).start())
+    spread_line(tr)
 
     scale = 1.0 / math.sqrt(channels)
     feature = jnp.dot(blocks[0].reshape(2 * cols, 128), wp[...], preferred_element_type=F32) + bias[...]
@@ -274,13 +304,49 @@
     high, low = split(dot_t(feature, wp[...]) * scale)
     queries = jnp.concatenate([high, low], axis=1)
 
-    others = keys.at[pl.ds(0, (devices - 1) * pooled_cols)]
-    pltpu.make_async_copy(others, others, all_recv.at[2]).wait()
-
-    across = col_tiles * pooled_cols
-    total_keys = devices * pooled_cols
+    query_out[...] = queries
+    offset_out[...] = jnp.broadcast_to(offset, offset_out.shape)
+
+    def forward(step):
+        row = lax.rem(tr + row_tiles - step, row_tiles)
+        block = keys.at[row, tc]
+        pltpu.make_async_copy(block, block, line_recv.at[row]).wait()
+        spread_line(row)
+
+    each(row_tiles, forward)
+    cross = keys.at[:, pl.ds(0, col_tiles - 1)]
+    pltpu.make_async_copy(cross, cross, all_recv.at[4]).wait()
+
+    for line in lines:
+        slot = line[2]
+
+        @pl.when(inside(line[0], 0))
+        def _(slot=slot):
+            pltpu.make_async_copy(edge_rows.at[slot], edge_rows.at[slot], row_send.at[slot]).wait()
+
+    for corner in corners:
+        slot = corner[3]
+
+        @pl.when(inside(corner[0], corner[1]))
+        def _(slot=slot):
+            pltpu.make_async_copy(edge_in.at[slot], edge_in.at[slot], edge_send.at[slot]).wait()
+
+    arrived(near_one, col_tiles - 1, all_send.at[0])
+    arrived(far_one, row_tiles - 1, all_send.at[1])
+    arrived(near_two, col_tiles - 1, all_send.at[2])
+    arrived(far_two, row_tiles - 1, all_send.at[3])
+    line = keys.at[pl.ds(0, row_tiles - 1), 0]
+    pltpu.make_async_copy(line, line, all_send.at[4]).wait()
+    pltpu.make_async_copy(cross, cross, all_send.at[5]).wait()
+
+
+def correlate(across, keys, query, offset_ref, o1, o2, o3, pool_b, pool_c):
+    total_keys = keys.shape[0]
     chunk = min(total_keys, 2048)
     lines1 = chunk // across
+    queries = query[...]
+    high = queries[:, 0:128]
+    offset = offset_ref[:, 0:1]
 
     def pooled(values, scratch, lines_in, width):
         pairs = jnp.sum(values.reshape(lines_in // 2, 2, width, 128), axis=1)
@@ -301,25 +367,6 @@
         o2[:, start // 4:(start + chunk) // 4] = fine(two).astype(BF16)
         three = pooled(two, pool_c, lines1 // 2, across // 2)
         o3[:, start // 16:(start + chunk) // 16] = fine(three).astype(BF16)
-
-    for line in lines:
-        slot = line[2]
-
-        @pl.when(inside(line[0], 0))
-        def _(slot=slot):
-            pltpu.make_async_copy(edge_rows.at[slot], edge_rows.at[slot], row_send.at[slot]).wait()
-
-    for corner in corners:
-        slot = corner[3]
-
-        @pl.when(inside(corner[0], corner[1]))
-        def _(slot=slot):
-            pltpu.make_async_copy(edge_in.at[slot], edge_in.at[slot], edge_send.at[slot]).wait()
-
-    for phase, slots in enumerate((stat_one, stat_two)):
-        gone = slots.at[pl.ds(0, devices - 1)]
-        pltpu.make_async_copy(gone, gone, all_send.at[phase]).wait()
-    pltpu.make_async_copy(others, others, all_send.at[2]).wait()
 
 
 def body(row_tiles, col_tiles, frame_one, frame_two, first_kernel, second_kernel, out_proj, out_bias):
@@ -333,12 +380,12 @@
     vmem = pltpu.VMEM
     anywhere = pl.BlockSpec(memory_space=pl.ANY)
     local = pl.BlockSpec(memory_space=pltpu.VMEM)
-    outs = pl.pallas_call(
+    key_blocks, query, offset = pl.pallas_call(
         functools.partial(kernel, row_tiles, col_tiles, rows, cols),
         out_shape=[
-            jax.ShapeDtypeStruct((queries, keys), BF16),
-            jax.ShapeDtypeStruct((queries, keys // 4), BF16),
-            jax.ShapeDtypeStruct((queries, keys // 16), BF16),
+            jax.ShapeDtypeStruct((row_tiles, col_tiles, cols // 2, cin), BF16),
+            jax.ShapeDtypeStruct((queries, 2 * cin), BF16),
+            jax.ShapeDtypeStruct((queries, 128), F32),
         ],
         in_specs=[anywhere] * 6,
         out_specs=[local] * 3,
@@ -357,28 +404,43 @@
             vmem((2, 2, wide, cin), F32),
             vmem((2, 4, cols + 32, cin), F32),
             vmem((2, 4, cols, 3 * cin), BF16),
-            vmem((devices, 4, cin), F32),
-            vmem((devices, 4, cin), F32),
-            vmem((keys, cin), BF16),
+            vmem((col_tiles, 4, cin), F32),
+            vmem((row_tiles, 4, cin), F32),
+            vmem((col_tiles, 4, cin), F32),
+            vmem((row_tiles, 4, cin), F32),
             vmem((cols, cin), F32),
-            vmem((chunk // 2, cin), F32),
-            vmem((chunk // 8, cin), F32),
             pltpu.SemaphoreType.DMA((6,)),
             pltpu.SemaphoreType.DMA((4,)),
             pltpu.SemaphoreType.DMA((4,)),
             pltpu.SemaphoreType.DMA((6,)),
             pltpu.SemaphoreType.DMA((6,)),
-            pltpu.SemaphoreType.DMA((3,)),
-            pltpu.SemaphoreType.DMA((3,)),
+            pltpu.SemaphoreType.DMA((6,)),
+            pltpu.SemaphoreType.DMA((5,)),
+            pltpu.SemaphoreType.DMA((row_tiles,)),
         ],
         compiler_params=pltpu.CompilerParams(
             collective_id=0, has_side_effects=True, vmem_limit_bytes=48 * 1024 * 1024
         ),
-    )(
-        frame_one, frame_two,
-        first_kernel.reshape(3, 3 * cin, cin), second_kernel.reshape(3, 3 * cin, cin),
-        out_proj, out_bias.reshape(1, channels),
-    )
+    )(*[
+        pltpu.with_memory_space_constraint(value, pltpu.HBM)
+        for value in (
+            frame_one, frame_two,
+            first_kernel.reshape(3, 3 * cin, cin), second_kernel.reshape(3, 3 * cin, cin),
+            out_proj, out_bias.reshape(1, channels),
+        )
+    ])
+    outs = pl.pallas_call(
+        functools.partial(correlate, col_tiles * cols // 2),
+        out_shape=[
+            jax.ShapeDtypeStruct((queries, keys), BF16),
+            jax.ShapeDtypeStruct((queries, keys // 4), BF16),
+            jax.ShapeDtypeStruct((queries, keys // 16), BF16),
+        ],
+        in_specs=[local] * 3,
+        out_specs=[local] * 3,
+        scratch_shapes=[vmem((chunk // 2, cin), F32), vmem((chunk // 8, cin), F32)],
+        compiler_params=pltpu.CompilerParams(vmem_limit_bytes=24 * 1024 * 1024),
+    )(key_blocks.reshape(keys, cin), query, offset)
     return tuple(out.reshape(rows, cols, -1) for out in outs)
 
 

time: 36.7 us -> 33.8 us (0.921)
  local copies, waits for them, and re-layouts: 6.9 us -> 0 us
  Pallas kernels: 28.7 us -> 33 us
    unnamed x15 -> x0, local copies, waits for them, and re-layouts: 6.9 us -> none
    pallas_call x1, Pallas kernels: 28.7 us -> 32 us  [body(): pl.pallas_call(functools.partial(kernel, row_tiles, col_tiles, rows, cols...]
    pallas_call x0 -> x1, Pallas kernels: none -> 1.04 us  [body(): pl.pallas_call(functools.partial(correlate, col_tiles * cols // 2), out_s...]
where the time goes in v2:
time: 33.8 us; the launch traced here: 33.7 us
  Pallas kernels  33 us (98%)
  between operations  0.64 us (2%)
    pallas_call x1, Pallas kernels, body(): pl.pallas_call(functools.partial(kernel, row_tiles, col_tiles, rows, cols...  32 us
    pallas_call x1, Pallas kernels, body(): pl.pallas_call(functools.partial(correlate, col_tiles * cols // 2), out_s...  1.04 us

profile of v2, /device:TPU:0, one launch (start us, length us, event | category | flops | bytes accessed | tf_op | source)
XLA Modules:
  0.0 33.7 jit_solution(4086850263159905860)
XLA Ops:
  0.6 32.0 %shard_map.85 = (bf16[8,4,32,128]{3,2,1,0:T(8,128)(2,1)S(1)}, bf16[128,256]{1,0:T(8,128)(2,1)S(1)}, f32[128,128]{1,0:T(8,128)S(1)}) custom-call(bf16[2,64,128]{2,1,0:T(8,128)(2,1)} %f1.1, bf16[2,64,128]{2,1,0:T(8,128)(2,1)} %f2.1, bf16[3,384,128]{2,1,0:T(8,128)(2,1)} %bitcast.8, bf16[3,384,128]{2,1,0:T(8,128)(2,1)} %bitcast.9, bf16[128,256]{1,0:T(8,128)(2,1)} %wp_hbm.1, ...), custom_call_target="tpu_custom_call" | custom-call | tf_op jit(solution)/shard_map/pallas_call | solution.py:383
  32.6 1.0 %shard_map.86 = (bf16[128,1024]{1,0:T(8,128)(2,1)}, bf16[128,256]{1,0:T(8,128)(2,1)}, bf16[128,64]{1,0:T(8,128)(2,1)}) custom-call(bf16[1024,128]{1,0:T(8,128)(2,1)S(1)} %bitcast.7, bf16[128,256]{1,0:T(8,128)(2,1)S(1)} %get-tuple-element.10.query, f32[128,128]{1,0:T(8,128)S(1)} %get-tuple-element.11.offset_ref), custom_call_target="tpu_custom_call" | custom-call | tf_op jit(solution)/shard_map/pallas_call | solution.py:432

commit v3 on v2

--- a/solution.py
+++ b/solution.py
@@ -30,8 +30,8 @@
     w1, w2, wp, bias,
     tiles, edge_rows, edge_out, edge_in,
     grid, patches, conv_own, conv_edge, hidden, patches2,
-    near_one, far_one, near_two, far_two, pool_a,
-    in_sem, row_send, row_recv, edge_send, edge_recv, all_send, all_recv, line_recv,
+    stat_one, stat_two, pool_a,
+    in_sem, row_send, row_recv, edge_send, edge_recv, all_send, all_recv,
 ):
     tr = lax.axis_index("tr")
     tc = lax.axis_index("tc")
@@ -60,37 +60,24 @@
         col = tc + side
         return (row >= 0) & (row < row_tiles) & (col >= 0) & (col < col_tiles)
 
-    def along_rows(step):
-        return (lax.rem(tr + step, row_tiles), tc)
-
-    def along_cols(step):
-        return (tr, lax.rem(tc + step, col_tiles))
-
-    def each(count, act):
-        if count <= 8:
-            for step in sorted(range(1, count), key=lambda s: min(s, count - s)):
-                act(step)
+    def each(act):
+        def turn(step, carried=0):
+            other = lax.rem(me + step, devices)
+            act((other // col_tiles, lax.rem(other, col_tiles)))
+            return carried
+
+        if devices <= 32:
+            for step in sorted(range(1, devices), key=lambda s: -min(s, devices - s)):
+                turn(step)
         else:
-            def turn(step, carried):
-                act(step)
-                return carried
-
-            lax.fori_loop(1, count, turn, 0)
+            lax.fori_loop(1, devices, turn, 0)
 
     barrier = pltpu.get_barrier_semaphore()
 
     def greet(place):
         pl.semaphore_signal(barrier, inc=1, device_id=place, device_id_type=MESH)
 
-    each(row_tiles, lambda step: greet(along_rows(step)))
-    each(col_tiles, lambda step: greet(along_cols(step)))
-    greeted = row_tiles + col_tiles - 2
-    for down, side in ((1, 1), (1, -1), (-1, 1), (-1, -1)):
-        @pl.when(inside(down, side))
-        def _(down=down, side=side):
-            greet((tr + down, tc + side))
-
-        greeted = greeted + inside(down, side).astype(jnp.int32)
+    each(greet)
 
     loads[0].wait()
     loads[1].wait()
@@ -104,7 +91,7 @@
             edge_out[0, line:line + 2, :] = values[0:2]
             edge_out[1, line:line + 2, :] = values[cols - 2:cols]
 
-    pl.semaphore_wait(barrier, greeted)
+    pl.semaphore_wait(barrier, devices - 1)
 
     corners = [
         (0, 1, 1, 0), (0, -1, 0, 1),
@@ -113,15 +100,12 @@
     ]
     lines = [(1, 1, 0), (-1, 0, 1), (1, 0, 2), (-1, 1, 3)]
 
-    def row_copies(down, row, slot):
-        return [
-            pltpu.make_async_remote_copy(
-                src_ref=frame.at[row], dst_ref=edge_rows.at[slot, f],
-                send_sem=row_send.at[slot], recv_sem=row_recv.at[slot],
-                device_id=(tr + down, tc), device_id_type=MESH,
-            )
-            for f, frame in enumerate((f1, f2))
-        ]
+    def row_copy(down, row, slot):
+        return pltpu.make_async_remote_copy(
+            src_ref=tiles.at[:, row], dst_ref=edge_rows.at[slot],
+            send_sem=row_send.at[slot], recv_sem=row_recv.at[slot],
+            device_id=(tr + down, tc), device_id_type=MESH,
+        )
 
     def edge_copy(down, side, which, slot):
         return pltpu.make_async_remote_copy(
@@ -133,8 +117,7 @@
     def send_row(line):
         @pl.when(inside(line[0], 0))
         def _():
-            for copy in row_copies(*line):
-                copy.start()
+            row_copy(*line).start()
 
     def send_edge(corner):
         @pl.when(inside(corner[0], corner[1]))
@@ -155,11 +138,9 @@
         def _():
             pltpu.make_async_copy(edge_in.at[slot], edge_in.at[slot], edge_recv.at[slot]).wait()
 
-    for line in lines[:2]:
-        send_row(line)
     for corner in corners:
         send_edge(corner)
-    for line in lines[2:]:
+    for line in lines:
         send_row(line)
 
     def fill_row(y, slot):
@@ -180,64 +161,64 @@
                 start = left - 9 + j
                 patches[f, y, :, j * 128:(j + 1) * 128] = grid[f, y, start:start + wide, :].astype(BF16)
 
+    def patch(first, *others):
+        parts = [patches[:, y].reshape(2 * wide, 384) for y in (first, *others)]
+        return parts[0] if len(parts) == 1 else jnp.concatenate(parts, axis=1)
+
+    def times(window, weights):
+        return jnp.dot(window, weights, preferred_element_type=F32)
+
+    def middle(weights):
+        return jnp.concatenate([weights[384:1152], weights[0:768]], axis=1)
+
+    for corner in corners[:2]:
+        await_edge(corner)
+    for y in range(2):
+        fill_edges(2 + y, 0, y)
+        fill_patches(2 + y)
+    loads[2].wait()
+    both = times(patch(2, 3), middle(w1))
     for line in lines[:2]:
         await_row(line)
-    for corner in corners:
+    for corner in corners[2:]:
         await_edge(corner)
     fill_row(1, 0)
     fill_row(4, 1)
     for y in range(2):
-        fill_edges(2 + y, 0, y)
         fill_edges(0 + y, 2, y)
         fill_edges(4 + y, 4, y)
-    for y in range(1, 5):
-        fill_patches(y)
-
-    loads[2].wait()
-
-    def convolve(first_row, count):
-        total = None
-        for i in range(3):
-            window = patches[:, first_row - 1 + i:first_row - 1 + i + count]
-            part = jnp.dot(window.reshape(2 * count * wide, 384), w1[i], preferred_element_type=F32)
-            total = part if total is None else total + part
-        return total.reshape(2, count, wide, 128)
-
-    def give(slots, mine, place, phase):
-        pltpu.make_async_remote_copy(
-            src_ref=slots.at[mine], dst_ref=slots.at[mine],
+    fill_patches(1)
+    fill_patches(4)
+    upper = both[:, 0:128] + times(patch(1), w1[0:384])
+    lower = both[:, 128:256] + times(patch(4), w1[768:1152])
+    conv_own[:, 0] = upper.reshape(2, wide, 128)
+    conv_own[:, 1] = lower.reshape(2, wide, 128)
+
+    def share(stats, slots, phase):
+        slots[me] = stats
+        each(lambda place: pltpu.make_async_remote_copy(
+            src_ref=slots.at[me], dst_ref=slots.at[me],
             send_sem=all_send.at[phase], recv_sem=all_recv.at[phase],
             device_id=place, device_id_type=MESH,
-        ).start()
-
-    def arrived(slots, count, sem):
-        others = slots.at[pl.ds(0, count)]
+        ).start())
+
+    def arrived(slots, sem):
+        others = slots.at[pl.ds(0, devices - 1)]
         pltpu.make_async_copy(others, others, sem).wait()
-
-    def share(stats, slots, phase):
-        slots[tc] = stats
-        each(col_tiles, lambda step: give(slots, tc, along_cols(step), phase))
-
-    def pass_on(near, far, phase):
-        arrived(near, col_tiles - 1, all_recv.at[phase])
-        far[tr] = jnp.sum(near[...], axis=0)
-        each(row_tiles, lambda step: give(far, tr, along_rows(step), phase + 1))
 
     def sums_of(values):
         total = jnp.sum(values, axis=(1, 2))
         squares = jnp.sum(values * values, axis=(1, 2))
         return jnp.concatenate([total, squares], axis=0)
 
-    def collect(far, phase):
-        arrived(far, row_tiles - 1, all_recv.at[phase])
-        total = jnp.sum(far[...], axis=0) / positions
+    def collect(slots, phase):
+        arrived(slots, all_recv.at[phase])
+        total = jnp.sum(slots[...], axis=0) / positions
         centre = total[0:2]
         spread = total[2:4] - centre * centre
         return centre[:, None, None, :], lax.rsqrt(spread + 1e-05)[:, None, None, :]
 
-    own = convolve(2, 2)
-    conv_own[...] = own
-    share(sums_of(own[:, :, 8:8 + cols]), near_one, 0)
+    share(sums_of(conv_own[:, :, 8:8 + cols]), stat_one, 0)
 
     for line in lines[2:]:
         await_row(line)
@@ -245,12 +226,11 @@
     fill_row(5, 3)
     fill_patches(0)
     fill_patches(5)
-    pass_on(near_one, far_one, 0)
-    conv_edge[:, 0:1] = convolve(1, 1)
-    conv_edge[:, 1:2] = convolve(4, 1)
+    conv_edge[:, 0] = times(patch(0, 1, 2), w1[...]).reshape(2, wide, 128)
+    conv_edge[:, 1] = times(patch(3, 4, 5), w1[...]).reshape(2, wide, 128)
     loads[3].wait()
 
-    centre, inverse = collect(far_one, 1)
+    centre, inverse = collect(stat_one, 0)
     spot = lax.broadcasted_iota(jnp.int32, (1, 1, wide, 128), 2)
     col_ok = ((spot >= 8) | (tc > 0)) & ((spot < 8 + cols) | (tc < col_tiles - 1))
 
@@ -265,37 +245,25 @@
             for j in range(3):
                 start = left - 1 + j
                 patches2[f, y, :, j * 128:(j + 1) * 128] = hidden[f, y, start:start + cols, :].astype(BF16)
-    second = None
-    for i in range(3):
-        window = patches2[:, i:i + 2].reshape(4 * cols, 384)
-        part = jnp.dot(window, w2[i], preferred_element_type=F32)
-        second = part if second is None else second + part
-    second = second.reshape(2, 2, cols, 128)
-    share(sums_of(second), near_two, 2)
+    lines2 = [patches2[:, y].reshape(2 * cols, 384) for y in range(4)]
+    both = times(jnp.concatenate(lines2[1:3], axis=1), middle(w2))
+    upper = both[:, 0:128] + times(lines2[0], w2[0:384])
+    lower = both[:, 128:256] + times(lines2[3], w2[768:1152])
+    second = jnp.stack([upper.reshape(2, cols, 128), lower.reshape(2, cols, 128)], axis=1)
+    share(sums_of(second), stat_two, 1)
     loads[4].wait()
     loads[5].wait()
-    pass_on(near_two, far_two, 2)
-    centre, inverse = collect(far_two, 3)
+    centre, inverse = collect(stat_two, 1)
     blocks = jax.nn.relu(tiles[...].astype(F32) + jax.nn.relu((second - centre) * inverse)).astype(BF16)
 
     pool_a[0:cols, :] = blocks[1, 0].astype(F32) + blocks[1, 1].astype(F32)
     small = (pool_a[pl.ds(0, pooled_cols, stride=2), :] + pool_a[pl.ds(1, pooled_cols, stride=2), :]) * 0.25
-    keys[tr, tc] = small.astype(BF16)
-
-    def key_copy(row, place, send_sem, recv_sem):
-        return pltpu.make_async_remote_copy(
-            src_ref=keys.at[row, tc], dst_ref=keys.at[row, tc],
-            send_sem=send_sem, recv_sem=recv_sem,
-            device_id=place, device_id_type=MESH,
-        )
-
-    def spread_line(row):
-        each(col_tiles, lambda step: key_copy(
-            row, along_cols(step), all_send.at[5], all_recv.at[4]).start())
-
-    each(row_tiles, lambda step: key_copy(
-        tr, along_rows(step), all_send.at[4], line_recv.at[tr]).start())
-    spread_line(tr)
+    keys[me] = small.astype(BF16)
+    each(lambda place: pltpu.make_async_remote_copy(
+        src_ref=keys.at[me], dst_ref=keys.at[me],
+        send_sem=all_send.at[2], recv_sem=all_recv.at[2],
+        device_id=place, device_id_type=MESH,
+    ).start())
 
     scale = 1.0 / math.sqrt(channels)
     feature = jnp.dot(blocks[0].reshape(2 * cols, 128), wp[...], preferred_element_type=F32) + bias[...]
@@ -307,15 +275,7 @@
     query_out[...] = queries
     offset_out[...] = jnp.broadcast_to(offset, offset_out.shape)
 
-    def forward(step):
-        row = lax.rem(tr + row_tiles - step, row_tiles)
-        block = keys.at[row, tc]
-        pltpu.make_async_copy(block, block, line_recv.at[row]).wait()
-        spread_line(row)
-
-    each(row_tiles, forward)
-    cross = keys.at[:, pl.ds(0, col_tiles - 1)]
-    pltpu.make_async_copy(cross, cross, all_recv.at[4]).wait()
+    arrived(keys, all_recv.at[2])
 
     for line in lines:
         slot = line[2]
@@ -331,13 +291,8 @@
         def _(slot=slot):
             pltpu.make_async_copy(edge_in.at[slot], edge_in.at[slot], edge_send.at[slot]).wait()
 
-    arrived(near_one, col_tiles - 1, all_send.at[0])
-    arrived(far_one, row_tiles - 1, all_send.at[1])
-    arrived(near_two, col_tiles - 1, all_send.at[2])
-    arrived(far_two, row_tiles - 1, all_send.at[3])
-    line = keys.at[pl.ds(0, row_tiles - 1), 0]
-    pltpu.make_async_copy(line, line, all_send.at[4]).wait()
-    pltpu.make_async_copy(cross, cross, all_send.at[5]).wait()
+    for phase, slots in enumerate((stat_one, stat_two, keys)):
+        arrived(slots, all_send.at[phase])
 
 
 def correlate(across, keys, query, offset_ref, o1, o2, o3, pool_b, pool_c):
@@ -383,15 +338,15 @@
     key_blocks, query, offset = pl.pallas_call(
         functools.partial(kernel, row_tiles, col_tiles, rows, cols),
         out_shape=[
-            jax.ShapeDtypeStruct((row_tiles, col_tiles, cols // 2, cin), BF16),
+            jax.ShapeDtypeStruct((devices, cols // 2, cin), BF16),
             jax.ShapeDtypeStruct((queries, 2 * cin), BF16),
             jax.ShapeDtypeStruct((queries, 128), F32),
         ],
         in_specs=[anywhere] * 6,
         out_specs=[local] * 3,
         scratch_shapes=[
-            vmem((3, 3 * cin, cin), BF16),
-            vmem((3, 3 * cin, cin), BF16),
+            vmem((9 * cin, cin), BF16),
+            vmem((9 * cin, cin), BF16),
             vmem((cin, channels), BF16),
             vmem((1, channels), F32),
             vmem((2, rows, cols, cin), BF16),
@@ -404,19 +359,16 @@
             vmem((2, 2, wide, cin), F32),
             vmem((2, 4, cols + 32, cin), F32),
             vmem((2, 4, cols, 3 * cin), BF16),
-            vmem((col_tiles, 4, cin), F32),
-            vmem((row_tiles, 4, cin), F32),
-            vmem((col_tiles, 4, cin), F32),
-            vmem((row_tiles, 4, cin), F32),
+            vmem((devices, 4, cin), F32),
+            vmem((devices, 4, cin), F32),
             vmem((cols, cin), F32),
             pltpu.SemaphoreType.DMA((6,)),
             pltpu.SemaphoreType.DMA((4,)),
             pltpu.SemaphoreType.DMA((4,)),
             pltpu.SemaphoreType.DMA((6,)),
             pltpu.SemaphoreType.DMA((6,)),
-            pltpu.SemaphoreType.DMA((6,)),
-            pltpu.SemaphoreType.DMA((5,)),
-            pltpu.SemaphoreType.DMA((row_tiles,)),
+            pltpu.SemaphoreType.DMA((3,)),
+            pltpu.SemaphoreType.DMA((3,)),
         ],
         compiler_params=pltpu.CompilerParams(
             collective_id=0, has_side_effects=True, vmem_limit_bytes=48 * 1024 * 1024
@@ -425,7 +377,7 @@
         pltpu.with_memory_space_constraint(value, pltpu.HBM)
         for value in (
             frame_one, frame_two,
-            first_kernel.reshape(3, 3 * cin, cin), second_kernel.reshape(3, 3 * cin, cin),
+            first_kernel.reshape(9 * cin, cin), second_kernel.reshape(9 * cin, cin),
             out_proj, out_bias.reshape(1, channels),
         )
     ])

time: 33.8 us -> 31.1 us (0.920)
  Pallas kernels: 33 us -> 30.3 us
    pallas_call x1, Pallas kernels: 32 us -> 29.2 us  [body(): pl.pallas_call(functools.partial(kernel, row_tiles, col_tiles, rows, cols...]
where the time goes in v3:
time: 31.1 us; the launch traced here: 30.9 us
  Pallas kernels  30.3 us (97%)
  between operations  0.64 us (2%)
    pallas_call x1, Pallas kernels, body(): pl.pallas_call(functools.partial(kernel, row_tiles, col_tiles, rows, cols...  29.2 us
    pallas_call x1, Pallas kernels, body(): pl.pallas_call(functools.partial(correlate, col_tiles * cols // 2), out_s...  1.04 us

profile of v3, /device:TPU:0, one launch (start us, length us, event | category | flops | bytes accessed | tf_op | source)
XLA Modules:
  0.0 30.9 jit_solution(15016087344718998768)
XLA Ops:
  0.6 29.2 %shard_map.85 = (bf16[32,32,128]{2,1,0:T(8,128)(2,1)S(1)}, bf16[128,256]{1,0:T(8,128)(2,1)S(1)}, f32[128,128]{1,0:T(8,128)S(1)}) custom-call(bf16[2,64,128]{2,1,0:T(8,128)(2,1)} %f1.1, bf16[2,64,128]{2,1,0:T(8,128)(2,1)} %f2.1, bf16[1152,128]{1,0:T(8,128)(2,1)} %bitcast.8, bf16[1152,128]{1,0:T(8,128)(2,1)} %bitcast.9, bf16[128,256]{1,0:T(8,128)(2,1)} %wp_hbm.1, ...), custom_call_target="tpu_custom_call" | custom-call | tf_op jit(solution)/shard_map/pallas_call | solution.py:338
  29.9 1.0 %shard_map.86 = (bf16[128,1024]{1,0:T(8,128)(2,1)}, bf16[128,256]{1,0:T(8,128)(2,1)}, bf16[128,64]{1,0:T(8,128)(2,1)}) custom-call(bf16[1024,128]{1,0:T(8,128)(2,1)S(1)} %bitcast.7, bf16[128,256]{1,0:T(8,128)(2,1)S(1)} %get-tuple-element.10.query, f32[128,128]{1,0:T(8,128)S(1)} %get-tuple-element.11.offset_ref), custom_call_target="tpu_custom_call" | custom-call | tf_op jit(solution)/shard_map/pallas_call | solution.py:384

commit v4 on v3

--- a/solution.py
+++ b/solution.py
@@ -9,6 +9,7 @@
 from jax.sharding import PartitionSpec as P
 
 MESH = pl.DeviceIdType.MESH
+FLAT = pl.DeviceIdType.LOGICAL
 F32 = jnp.float32
 BF16 = jnp.bfloat16
 
@@ -29,8 +30,8 @@
     keys, query_out, offset_out,
     w1, w2, wp, bias,
     tiles, edge_rows, edge_out, edge_in,
-    grid, patches, conv_own, conv_edge, hidden, patches2,
-    stat_one, stat_two, pool_a,
+    grid, patches, conv, hidden, patches2, conv2,
+    stats, pool_a,
     in_sem, row_send, row_recv, edge_send, edge_recv, all_send, all_recv,
 ):
     tr = lax.axis_index("tr")
@@ -60,24 +61,28 @@
         col = tc + side
         return (row >= 0) & (row < row_tiles) & (col >= 0) & (col < col_tiles)
 
-    def each(act):
+    far_first = sorted(range(1, devices), key=lambda s: -min(s, devices - s))
+    close = (1, col_tiles - 1, col_tiles, col_tiles + 1)
+    close_first = sorted(far_first, key=lambda s: min(s, devices - s) not in close)
+
+    def each(act, order):
         def turn(step, carried=0):
-            other = lax.rem(me + step, devices)
-            act((other // col_tiles, lax.rem(other, col_tiles)))
+            other = me + step
+            act(jnp.where(other < devices, other, other - devices))
             return carried
 
         if devices <= 32:
-            for step in sorted(range(1, devices), key=lambda s: -min(s, devices - s)):
+            for step in order:
                 turn(step)
         else:
             lax.fori_loop(1, devices, turn, 0)
 
     barrier = pltpu.get_barrier_semaphore()
 
-    def greet(place):
-        pl.semaphore_signal(barrier, inc=1, device_id=place, device_id_type=MESH)
-
-    each(greet)
+    def greet(index):
+        pl.semaphore_signal(barrier, inc=1, device_id=index, device_id_type=FLAT)
+
+    each(greet, close_first)
 
     loads[0].wait()
     loads[1].wait()
@@ -143,27 +148,23 @@
     for line in lines:
         send_row(line)
 
-    def fill_row(y, slot):
-        for f in range(2):
-            grid[f, y, left:right, :] = edge_rows[slot, f].astype(F32)
-
-    def fill_edges(y, slot, base):
-        for f in range(2):
-            line = f * 4 + base * 2
-            grid[f, y, left - 2:left, :] = edge_in[slot, line:line + 2, :]
-            grid[f, y, right:right + 2, :] = edge_in[slot + 1, line:line + 2, :]
-
     wide = cols + 16
 
-    def fill_patches(y):
-        for f in range(2):
-            for j in range(3):
-                start = left - 9 + j
-                patches[f, y, :, j * 128:(j + 1) * 128] = grid[f, y, start:start + wide, :].astype(BF16)
-
-    def patch(first, *others):
-        parts = [patches[:, y].reshape(2 * wide, 384) for y in (first, *others)]
-        return parts[0] if len(parts) == 1 else jnp.concatenate(parts, axis=1)
+    def fill_row(f, y, slot):
+        grid[f, y, left:right, :] = edge_rows[slot, f].astype(F32)
+
+    def fill_edges(f, y, slot, base):
+        line = f * 4 + base * 2
+        grid[f, y, left - 2:left, :] = edge_in[slot, line:line + 2, :]
+        grid[f, y, right:right + 2, :] = edge_in[slot + 1, line:line + 2, :]
+
+    def fill_patches(f, y):
+        for j in range(3):
+            start = left - 9 + j
+            patches[f, y, :, j * 128:(j + 1) * 128] = grid[f, y, start:start + wide, :].astype(BF16)
+
+    def patch(source, f, *lines_in):
+        return jnp.concatenate([source[f, y] for y in lines_in], axis=1)
 
     def times(window, weights):
         return jnp.dot(window, weights, preferred_element_type=F32)
@@ -171,102 +172,109 @@
     def middle(weights):
         return jnp.concatenate([weights[384:1152], weights[0:768]], axis=1)
 
+    def send_block(slots, phase):
+        each(lambda index: pltpu.make_async_remote_copy(
+            src_ref=slots.at[me], dst_ref=slots.at[me],
+            send_sem=all_send.at[phase], recv_sem=all_recv.at[phase],
+            device_id=index, device_id_type=FLAT,
+        ).start(), far_first)
+
+    def arrived(slots, sem):
+        others = slots.at[pl.ds(0, devices - 1)]
+        pltpu.make_async_copy(others, others, sem).wait()
+
+    def share(upper, lower, phase):
+        total = jnp.sum(upper + lower, axis=0, keepdims=True)
+        squares = jnp.sum(upper * upper + lower * lower, axis=0, keepdims=True)
+        stats[phase, me] = jnp.concatenate([total, squares], axis=0)
+        send_block(stats.at[phase], phase)
+
+    def collect(phase):
+        arrived(stats.at[phase], all_recv.at[phase])
+        total = jnp.sum(stats[phase], axis=0) / positions
+        centre = total[0:1]
+        spread = total[1:2] - centre * centre
+        return centre, lax.rsqrt(spread + 1e-05)
+
+    spot = lax.broadcasted_iota(jnp.int32, (wide, 128), 0)
+    col_ok = ((spot >= 8) | (tc > 0)) & ((spot < 8 + cols) | (tc < col_tiles - 1))
+    row_ok = (col_ok & (tr > 0), col_ok, col_ok, col_ok & (tr < row_tiles - 1))
+
+    def start_own(f):
+        for y in range(2):
+            fill_edges(f, 2 + y, 0, y)
+            fill_patches(f, 2 + y)
+        return times(patch(patches, f, 2, 3), middle(w1))
+
+    def finish_own(f, both):
+        fill_row(f, 1, 0)
+        fill_row(f, 4, 1)
+        for y in range(2):
+            fill_edges(f, 0 + y, 2, y)
+            fill_edges(f, 4 + y, 4, y)
+        fill_patches(f, 1)
+        fill_patches(f, 4)
+        conv[f, 1] = both[:, 0:128] + times(patches[f, 1], w1[0:384])
+        conv[f, 2] = both[:, 128:256] + times(patches[f, 4], w1[768:1152])
+        share(conv[f, 1, 8:8 + cols], conv[f, 2, 8:8 + cols], f)
+
+    def edge_lines(f):
+        fill_row(f, 0, 2)
+        fill_row(f, 5, 3)
+        fill_patches(f, 0)
+        fill_patches(f, 5)
+        conv[f, 0] = times(patch(patches, f, 0, 1, 2), w1[...])
+        conv[f, 3] = times(patch(patches, f, 3, 4, 5), w1[...])
+
+    def second_half(f):
+        centre, inverse = collect(f)
+        for y in range(4):
+            values = jax.nn.relu((conv[f, y] - centre) * inverse)
+            hidden[f, y, 8:8 + wide, :] = jnp.where(row_ok[y], values, 0.0)
+            for j in range(3):
+                start = left - 1 + j
+                patches2[f, y, :, j * 128:(j + 1) * 128] = hidden[f, y, start:start + cols, :].astype(BF16)
+        both = times(patch(patches2, f, 1, 2), middle(w2))
+        upper = both[:, 0:128] + times(patches2[f, 0], w2[0:384])
+        lower = both[:, 128:256] + times(patches2[f, 3], w2[768:1152])
+        share(upper, lower, 2 + f)
+        conv2[f, 0] = upper
+        conv2[f, 1] = lower
+
+    def blocks_of(f):
+        centre, inverse = collect(2 + f)
+        values = jax.nn.relu((conv2[f] - centre) * inverse)
+        return jax.nn.relu(tiles[f].astype(F32) + values).astype(BF16)
+
     for corner in corners[:2]:
         await_edge(corner)
-    for y in range(2):
-        fill_edges(2 + y, 0, y)
-        fill_patches(2 + y)
     loads[2].wait()
-    both = times(patch(2, 3), middle(w1))
+    both = start_own(1)
     for line in lines[:2]:
         await_row(line)
     for corner in corners[2:]:
         await_edge(corner)
-    fill_row(1, 0)
-    fill_row(4, 1)
-    for y in range(2):
-        fill_edges(0 + y, 2, y)
-        fill_edges(4 + y, 4, y)
-    fill_patches(1)
-    fill_patches(4)
-    upper = both[:, 0:128] + times(patch(1), w1[0:384])
-    lower = both[:, 128:256] + times(patch(4), w1[768:1152])
-    conv_own[:, 0] = upper.reshape(2, wide, 128)
-    conv_own[:, 1] = lower.reshape(2, wide, 128)
-
-    def share(stats, slots, phase):
-        slots[me] = stats
-        each(lambda place: pltpu.make_async_remote_copy(
-            src_ref=slots.at[me], dst_ref=slots.at[me],
-            send_sem=all_send.at[phase], recv_sem=all_recv.at[phase],
-            device_id=place, device_id_type=MESH,
-        ).start())
-
-    def arrived(slots, sem):
-        others = slots.at[pl.ds(0, devices - 1)]
-        pltpu.make_async_copy(others, others, sem).wait()
-
-    def sums_of(values):
-        total = jnp.sum(values, axis=(1, 2))
-        squares = jnp.sum(values * values, axis=(1, 2))
-        return jnp.concatenate([total, squares], axis=0)
-
-    def collect(slots, phase):
-        arrived(slots, all_recv.at[phase])
-        total = jnp.sum(slots[...], axis=0) / positions
-        centre = total[0:2]
-        spread = total[2:4] - centre * centre
-        return centre[:, None, None, :], lax.rsqrt(spread + 1e-05)[:, None, None, :]
-
-    share(sums_of(conv_own[:, :, 8:8 + cols]), stat_one, 0)
-
+    finish_own(1, both)
+    finish_own(0, start_own(0))
     for line in lines[2:]:
         await_row(line)
-    fill_row(0, 2)
-    fill_row(5, 3)
-    fill_patches(0)
-    fill_patches(5)
-    conv_edge[:, 0] = times(patch(0, 1, 2), w1[...]).reshape(2, wide, 128)
-    conv_edge[:, 1] = times(patch(3, 4, 5), w1[...]).reshape(2, wide, 128)
+    edge_lines(1)
     loads[3].wait()
-
-    centre, inverse = collect(stat_one, 0)
-    spot = lax.broadcasted_iota(jnp.int32, (1, 1, wide, 128), 2)
-    col_ok = ((spot >= 8) | (tc > 0)) & ((spot < 8 + cols) | (tc < col_tiles - 1))
-
-    def normal(values, keep):
-        return jnp.where(keep, jax.nn.relu((values - centre) * inverse), 0.0)
-
-    hidden[:, 1:3, 8:8 + wide, :] = normal(conv_own[...], col_ok)
-    hidden[:, 0:1, 8:8 + wide, :] = normal(conv_edge[:, 0:1], col_ok & (tr > 0))
-    hidden[:, 3:4, 8:8 + wide, :] = normal(conv_edge[:, 1:2], col_ok & (tr < row_tiles - 1))
-    for f in range(2):
-        for y in range(4):
-            for j in range(3):
-                start = left - 1 + j
-                patches2[f, y, :, j * 128:(j + 1) * 128] = hidden[f, y, start:start + cols, :].astype(BF16)
-    lines2 = [patches2[:, y].reshape(2 * cols, 384) for y in range(4)]
-    both = times(jnp.concatenate(lines2[1:3], axis=1), middle(w2))
-    upper = both[:, 0:128] + times(lines2[0], w2[0:384])
-    lower = both[:, 128:256] + times(lines2[3], w2[768:1152])
-    second = jnp.stack([upper.reshape(2, cols, 128), lower.reshape(2, cols, 128)], axis=1)
-    share(sums_of(second), stat_two, 1)
+    second_half(1)
+    edge_lines(0)
+    second_half(0)
+    block = blocks_of(1)
+
+    pool_a[0:cols, :] = block[0].astype(F32) + block[1].astype(F32)
+    small = (pool_a[pl.ds(0, pooled_cols, stride=2), :] + pool_a[pl.ds(1, pooled_cols, stride=2), :]) * 0.25
+    keys[me] = small.astype(BF16)
+    send_block(keys, 4)
+
     loads[4].wait()
     loads[5].wait()
-    centre, inverse = collect(stat_two, 1)
-    blocks = jax.nn.relu(tiles[...].astype(F32) + jax.nn.relu((second - centre) * inverse)).astype(BF16)
-
-    pool_a[0:cols, :] = blocks[1, 0].astype(F32) + blocks[1, 1].astype(F32)
-    small = (pool_a[pl.ds(0, pooled_cols, stride=2), :] + pool_a[pl.ds(1, pooled_cols, stride=2), :]) * 0.25
-    keys[me] = small.astype(BF16)
-    each(lambda place: pltpu.make_async_remote_copy(
-        src_ref=keys.at[me], dst_ref=keys.at[me],
-        send_sem=all_send.at[2], recv_sem=all_recv.at[2],
-        device_id=place, device_id_type=MESH,
-    ).start())
-
+    block = blocks_of(0)
     scale = 1.0 / math.sqrt(channels)
-    feature = jnp.dot(blocks[0].reshape(2 * cols, 128), wp[...], preferred_element_type=F32) + bias[...]
+    feature = jnp.dot(block.reshape(2 * cols, 128), wp[...], preferred_element_type=F32) + bias[...]
     feature = feature.astype(BF16)
     offset = jnp.sum(feature.astype(F32) * bias[...], axis=1, keepdims=True) * scale
     high, low = split(dot_t(feature, wp[...]) * scale)
@@ -275,7 +283,7 @@
     query_out[...] = queries
     offset_out[...] = jnp.broadcast_to(offset, offset_out.shape)
 
-    arrived(keys, all_recv.at[2])
+    arrived(keys, all_recv.at[4])
 
     for line in lines:
         slot = line[2]
@@ -291,8 +299,9 @@
         def _(slot=slot):
             pltpu.make_async_copy(edge_in.at[slot], edge_in.at[slot], edge_send.at[slot]).wait()
 
-    for phase, slots in enumerate((stat_one, stat_two, keys)):
-        arrived(slots, all_send.at[phase])
+    for phase in range(4):
+        arrived(stats.at[phase], all_send.at[phase])
+    arrived(keys, all_send.at[4])
 
 
 def correlate(across, keys, query, offset_ref, o1, o2, o3, pool_b, pool_c):
@@ -355,20 +364,19 @@
             vmem((6, 8, cin), F32),
             vmem((2, 6, cols + 32, cin), F32),
             vmem((2, 6, wide, 3 * cin), BF16),
-            vmem((2, 2, wide, cin), F32),
-            vmem((2, 2, wide, cin), F32),
+            vmem((2, 4, wide, cin), F32),
             vmem((2, 4, cols + 32, cin), F32),
             vmem((2, 4, cols, 3 * cin), BF16),
-            vmem((devices, 4, cin), F32),
-            vmem((devices, 4, cin), F32),
+            vmem((2, rows, cols, cin), F32),
+            vmem((4, devices, 2, cin), F32),
             vmem((cols, cin), F32),
             pltpu.SemaphoreType.DMA((6,)),
             pltpu.SemaphoreType.DMA((4,)),
             pltpu.SemaphoreType.DMA((4,)),
             pltpu.SemaphoreType.DMA((6,)),
             pltpu.SemaphoreType.DMA((6,)),
-            pltpu.SemaphoreType.DMA((3,)),
-            pltpu.SemaphoreType.DMA((3,)),
+            pltpu.SemaphoreType.DMA((5,)),
+            pltpu.SemaphoreType.DMA((5,)),
         ],
         compiler_params=pltpu.CompilerParams(
             collective_id=0, has_side_effects=True, vmem_limit_bytes=48 * 1024 * 1024

time: 31.1 us -> 30.7 us (0.987)
  Pallas kernels: 30.3 us -> 29.9 us
    pallas_call x1, Pallas kernels: 29.2 us -> 28.8 us  [body(): pl.pallas_call(functools.partial(kernel, row_tiles, col_tiles, rows, cols...]
where the time goes in v4:
time: 30.7 us; the launch traced here: 30.5 us
  Pallas kernels  29.9 us (97%)
  between operations  0.64 us (2%)
    pallas_call x1, Pallas kernels, body(): pl.pallas_call(functools.partial(kernel, row_tiles, col_tiles, rows, cols...  28.8 us
    pallas_call x1, Pallas kernels, body(): pl.pallas_call(functools.partial(correlate, col_tiles * cols // 2), out_s...  1.04 us

profile of v4, /device:TPU:0, one launch (start us, length us, event | category | flops | bytes accessed | tf_op | source)
XLA Modules:
  0.0 30.5 jit_solution(12127749252614001604)
XLA Ops:
  0.6 28.8 %shard_map.85 = (bf16[32,32,128]{2,1,0:T(8,128)(2,1)S(1)}, bf16[128,256]{1,0:T(8,128)(2,1)S(1)}, f32[128,128]{1,0:T(8,128)S(1)}) custom-call(bf16[2,64,128]{2,1,0:T(8,128)(2,1)} %f1.1, bf16[2,64,128]{2,1,0:T(8,128)(2,1)} %f2.1, bf16[1152,128]{1,0:T(8,128)(2,1)} %bitcast.8, bf16[1152,128]{1,0:T(8,128)(2,1)} %bitcast.9, bf16[128,256]{1,0:T(8,128)(2,1)} %wp_hbm.1, ...), custom_call_target="tpu_custom_call" | custom-call | tf_op jit(solution)/shard_map/pallas_call | solution.py:347
  29.5 1.0 %shard_map.86 = (bf16[128,1024]{1,0:T(8,128)(2,1)}, bf16[128,256]{1,0:T(8,128)(2,1)}, bf16[128,64]{1,0:T(8,128)(2,1)}) custom-call(bf16[1024,128]{1,0:T(8,128)(2,1)S(1)} %bitcast.7, bf16[128,256]{1,0:T(8,128)(2,1)S(1)} %get-tuple-element.10.query, f32[128,128]{1,0:T(8,128)S(1)} %get-tuple-element.11.offset_ref), custom_call_target="tpu_custom_call" | custom-call | tf_op jit(solution)/shard_map/pallas_call | solution.py:392

commit v5 on v4

--- a/solution.py
+++ b/solution.py
@@ -32,7 +32,7 @@
     tiles, edge_rows, edge_out, edge_in,
     grid, patches, conv, hidden, patches2, conv2,
     stats, pool_a,
-    in_sem, row_send, row_recv, edge_send, edge_recv, all_send, all_recv,
+    in_sem, row_send, row_recv, edge_send, edge_recv, all_send, all_recv, key_recv,
 ):
     tr = lax.axis_index("tr")
     tc = lax.axis_index("tc")
@@ -65,10 +65,12 @@
     close = (1, col_tiles - 1, col_tiles, col_tiles + 1)
     close_first = sorted(far_first, key=lambda s: min(s, devices - s) not in close)
 
+    def wrap(index):
+        return jnp.where(index < devices, index, index - devices)
+
     def each(act, order):
         def turn(step, carried=0):
-            other = me + step
-            act(jnp.where(other < devices, other, other - devices))
+            act(wrap(me + step))
             return carried
 
         if devices <= 32:
@@ -105,10 +107,10 @@
     ]
     lines = [(1, 1, 0), (-1, 0, 1), (1, 0, 2), (-1, 1, 3)]
 
-    def row_copy(down, row, slot):
+    def row_copy(f, down, row, slot):
         return pltpu.make_async_remote_copy(
-            src_ref=tiles.at[:, row], dst_ref=edge_rows.at[slot],
-            send_sem=row_send.at[slot], recv_sem=row_recv.at[slot],
+            src_ref=tiles.at[f, row], dst_ref=edge_rows.at[slot, f],
+            send_sem=row_send.at[slot, f], recv_sem=row_recv.at[slot, f],
             device_id=(tr + down, tc), device_id_type=MESH,
         )
 
@@ -119,22 +121,22 @@
             device_id=(tr + down, tc + side), device_id_type=MESH,
         )
 
-    def send_row(line):
+    def send_row(f, line):
         @pl.when(inside(line[0], 0))
         def _():
-            row_copy(*line).start()
+            row_copy(f, *line).start()
 
     def send_edge(corner):
         @pl.when(inside(corner[0], corner[1]))
         def _():
             edge_copy(*corner).start()
 
-    def await_row(line):
-        slot = line[2]
+    def await_row(f, line):
+        landed = edge_rows.at[line[2], f]
 
         @pl.when(inside(-line[0], 0))
         def _():
-            pltpu.make_async_copy(edge_rows.at[slot], edge_rows.at[slot], row_recv.at[slot]).wait()
+            pltpu.make_async_copy(landed, landed, row_recv.at[line[2], f]).wait()
 
     def await_edge(corner):
         slot = corner[3]
@@ -145,8 +147,10 @@
 
     for corner in corners:
         send_edge(corner)
-    for line in lines:
-        send_row(line)
+    for pair in (lines[:2], lines[2:]):
+        for f in (1, 0):
+            for line in pair:
+                send_row(f, line)
 
     wide = cols + 16
 
@@ -251,16 +255,21 @@
     loads[2].wait()
     both = start_own(1)
     for line in lines[:2]:
-        await_row(line)
+        await_row(1, line)
     for corner in corners[2:]:
         await_edge(corner)
     finish_own(1, both)
-    finish_own(0, start_own(0))
+    both = start_own(0)
+    for line in lines[:2]:
+        await_row(0, line)
+    finish_own(0, both)
     for line in lines[2:]:
-        await_row(line)
+        await_row(1, line)
     edge_lines(1)
     loads[3].wait()
     second_half(1)
+    for line in lines[2:]:
+        await_row(0, line)
     edge_lines(0)
     second_half(0)
     block = blocks_of(1)
@@ -268,7 +277,42 @@
     pool_a[0:cols, :] = block[0].astype(F32) + block[1].astype(F32)
     small = (pool_a[pl.ds(0, pooled_cols, stride=2), :] + pool_a[pl.ds(1, pooled_cols, stride=2), :]) * 0.25
     keys[me] = small.astype(BF16)
-    send_block(keys, 4)
+    sibling = jnp.where(lax.rem(tc, 2) == 0, me + 1, me - 1)
+    chips = devices // 2
+
+    def hand_over(block):
+        pltpu.make_async_remote_copy(
+            src_ref=keys.at[block], dst_ref=keys.at[block],
+            send_sem=all_send.at[5], recv_sem=all_recv.at[5],
+            device_id=sibling, device_id_type=FLAT,
+        ).start()
+
+    def send_key(hop):
+        pltpu.make_async_remote_copy(
+            src_ref=keys.at[me], dst_ref=keys.at[me],
+            send_sem=all_send.at[4], recv_sem=key_recv.at[hop],
+            device_id=wrap(me + 2 * hop), device_id_type=FLAT,
+        ).start()
+
+    def pass_key(hop):
+        block = wrap(me + devices - 2 * hop)
+        pltpu.make_async_copy(keys.at[block], keys.at[block], key_recv.at[hop]).wait()
+        hand_over(block)
+
+    def each_chip(act, order):
+        def turn(hop, carried=0):
+            act(hop)
+            return carried
+
+        if chips <= 16:
+            for hop in order:
+                turn(hop)
+        else:
+            lax.fori_loop(1, chips, turn, 0)
+
+    far_chips = sorted(range(1, chips), key=lambda h: -min(h, chips - h))
+    each_chip(send_key, far_chips)
+    hand_over(me)
 
     loads[4].wait()
     loads[5].wait()
@@ -283,14 +327,16 @@
     query_out[...] = queries
     offset_out[...] = jnp.broadcast_to(offset, offset_out.shape)
 
-    arrived(keys, all_recv.at[4])
+    each_chip(pass_key, far_chips[::-1])
+    handed = keys.at[pl.ds(0, chips)]
+    pltpu.make_async_copy(handed, handed, all_recv.at[5]).wait()
 
     for line in lines:
-        slot = line[2]
-
-        @pl.when(inside(line[0], 0))
-        def _(slot=slot):
-            pltpu.make_async_copy(edge_rows.at[slot], edge_rows.at[slot], row_send.at[slot]).wait()
+        for f in range(2):
+            @pl.when(inside(line[0], 0))
+            def _(slot=line[2], f=f):
+                gone = edge_rows.at[slot, f]
+                pltpu.make_async_copy(gone, gone, row_send.at[slot, f]).wait()
 
     for corner in corners:
         slot = corner[3]
@@ -301,7 +347,9 @@
 
     for phase in range(4):
         arrived(stats.at[phase], all_send.at[phase])
-    arrived(keys, all_send.at[4])
+    sent = keys.at[pl.ds(0, chips - 1)]
+    pltpu.make_async_copy(sent, sent, all_send.at[4]).wait()
+    pltpu.make_async_copy(handed, handed, all_send.at[5]).wait()
 
 
 def correlate(across, keys, query, offset_ref, o1, o2, o3, pool_b, pool_c):
@@ -371,12 +419,13 @@
             vmem((4, devices, 2, cin), F32),
             vmem((cols, cin), F32),
             pltpu.SemaphoreType.DMA((6,)),
-            pltpu.SemaphoreType.DMA((4,)),
-            pltpu.SemaphoreType.DMA((4,)),
+            pltpu.SemaphoreType.DMA((4, 2)),
+            pltpu.SemaphoreType.DMA((4, 2)),
             pltpu.SemaphoreType.DMA((6,)),
             pltpu.SemaphoreType.DMA((6,)),
-            pltpu.SemaphoreType.DMA((5,)),
-            pltpu.SemaphoreType.DMA((5,)),
+            pltpu.SemaphoreType.DMA((6,)),
+            pltpu.SemaphoreType.DMA((6,)),
+            pltpu.SemaphoreType.DMA((devices // 2,)),
         ],
         compiler_params=pltpu.CompilerParams(
             collective_id=0, has_side_effects=True, vmem_limit_bytes=48 * 1024 * 1024

time: 30.7 us -> 28.8 us (0.938)
  Pallas kernels: 29.9 us -> 28.1 us
    pallas_call x1, Pallas kernels: 28.8 us -> 27 us  [body(): pl.pallas_call(functools.partial(kernel, row_tiles, col_tiles, rows, cols...]
where the time goes in v5:
time: 28.8 us; the launch traced here: 28.7 us
  Pallas kernels  28.1 us (98%)
  between operations  0.64 us (2%)
    pallas_call x1, Pallas kernels, body(): pl.pallas_call(functools.partial(kernel, row_tiles, col_tiles, rows, cols...  27 us
    pallas_call x1, Pallas kernels, body(): pl.pallas_call(functools.partial(correlate, col_tiles * cols // 2), out_s...  1.04 us

profile of v5, /device:TPU:0, one launch (start us, length us, event | category | flops | bytes accessed | tf_op | source)
XLA Modules:
  0.0 28.7 jit_solution(188406765813745742)
XLA Ops:
  0.6 27.0 %shard_map.85 = (bf16[32,32,128]{2,1,0:T(8,128)(2,1)S(1)}, bf16[128,256]{1,0:T(8,128)(2,1)S(1)}, f32[128,128]{1,0:T(8,128)S(1)}) custom-call(bf16[2,64,128]{2,1,0:T(8,128)(2,1)} %f1.1, bf16[2,64,128]{2,1,0:T(8,128)(2,1)} %f2.1, bf16[1152,128]{1,0:T(8,128)(2,1)} %bitcast.8, bf16[1152,128]{1,0:T(8,128)(2,1)} %bitcast.9, bf16[128,256]{1,0:T(8,128)(2,1)} %wp_hbm.1, ...), custom_call_target="tpu_custom_call" | custom-call | tf_op jit(solution)/shard_map/pallas_call | solution.py:395
  27.7 1.0 %shard_map.86 = (bf16[128,1024]{1,0:T(8,128)(2,1)}, bf16[128,256]{1,0:T(8,128)(2,1)}, bf16[128,64]{1,0:T(8,128)(2,1)}) custom-call(bf16[1024,128]{1,0:T(8,128)(2,1)S(1)} %bitcast.7, bf16[128,256]{1,0:T(8,128)(2,1)S(1)} %get-tuple-element.10.query, f32[128,128]{1,0:T(8,128)S(1)} %get-tuple-element.11.offset_ref), custom_call_target="tpu_custom_call" | custom-call | tf_op jit(solution)/shard_map/pallas_call | solution.py:441

commit v6 on v5

--- a/solution.py
+++ b/solution.py
@@ -61,30 +61,33 @@
         col = tc + side
         return (row >= 0) & (row < row_tiles) & (col >= 0) & (col < col_tiles)
 
-    far_first = sorted(range(1, devices), key=lambda s: -min(s, devices - s))
-    close = (1, col_tiles - 1, col_tiles, col_tiles + 1)
-    close_first = sorted(far_first, key=lambda s: min(s, devices - s) not in close)
-
     def wrap(index):
         return jnp.where(index < devices, index, index - devices)
 
-    def each(act, order):
-        def turn(step, carried=0):
-            act(wrap(me + step))
+    def around(count, act, near):
+        half = count // 2
+
+        def turn(turn_index, carried):
+            step = turn_index if near else half - turn_index
+            act(step)
+            act(count - step)
             return carried
 
-        if devices <= 32:
-            for step in order:
-                turn(step)
-        else:
-            lax.fori_loop(1, devices, turn, 0)
+        if not near:
+            act(half)
+        lax.fori_loop(1, half, turn, 0)
+        if near:
+            act(half)
+
+    def each(act, near=False):
+        around(devices, lambda step: act(wrap(me + step)), near)
 
     barrier = pltpu.get_barrier_semaphore()
 
     def greet(index):
         pl.semaphore_signal(barrier, inc=1, device_id=index, device_id_type=FLAT)
 
-    each(greet, close_first)
+    each(greet, near=True)
 
     loads[0].wait()
     loads[1].wait()
@@ -181,7 +184,7 @@
             src_ref=slots.at[me], dst_ref=slots.at[me],
             send_sem=all_send.at[phase], recv_sem=all_recv.at[phase],
             device_id=index, device_id_type=FLAT,
-        ).start(), far_first)
+        ).start())
 
     def arrived(slots, sem):
         others = slots.at[pl.ds(0, devices - 1)]
@@ -299,19 +302,7 @@
         pltpu.make_async_copy(keys.at[block], keys.at[block], key_recv.at[hop]).wait()
         hand_over(block)
 
-    def each_chip(act, order):
-        def turn(hop, carried=0):
-            act(hop)
-            return carried
-
-        if chips <= 16:
-            for hop in order:
-                turn(hop)
-        else:
-            lax.fori_loop(1, chips, turn, 0)
-
-    far_chips = sorted(range(1, chips), key=lambda h: -min(h, chips - h))
-    each_chip(send_key, far_chips)
+    around(chips, send_key, near=False)
     hand_over(me)
 
     loads[4].wait()
@@ -327,7 +318,7 @@
     query_out[...] = queries
     offset_out[...] = jnp.broadcast_to(offset, offset_out.shape)
 
-    each_chip(pass_key, far_chips[::-1])
+    around(chips, pass_key, near=True)
     handed = keys.at[pl.ds(0, chips)]
     pltpu.make_async_copy(handed, handed, all_recv.at[5]).wait()
 

time: 28.8 us -> 29 us (level)
  no operation moved by 1% of the time
where the time goes in v6:
time: 29 us; the launch traced here: 28.9 us
  Pallas kernels  28.2 us (97%)
  between operations  0.64 us (2%)
    pallas_call x1, Pallas kernels, body(): pl.pallas_call(functools.partial(kernel, row_tiles, col_tiles, rows, cols...  27.2 us
    pallas_call x1, Pallas kernels, body(): pl.pallas_call(functools.partial(correlate, col_tiles * cols // 2), out_s...  1.04 us

profile of v6, /device:TPU:0, one launch (start us, length us, event | category | flops | bytes accessed | tf_op | source)
XLA Modules:
  0.0 28.9 jit_solution(11210492162997614943)
XLA Ops:
  0.6 27.2 %shard_map.85 = (bf16[32,32,128]{2,1,0:T(8,128)(2,1)S(1)}, bf16[128,256]{1,0:T(8,128)(2,1)S(1)}, f32[128,128]{1,0:T(8,128)S(1)}) custom-call(bf16[2,64,128]{2,1,0:T(8,128)(2,1)} %f1.1, bf16[2,64,128]{2,1,0:T(8,128)(2,1)} %f2.1, bf16[1152,128]{1,0:T(8,128)(2,1)} %bitcast.8, bf16[1152,128]{1,0:T(8,128)(2,1)} %bitcast.9, bf16[128,256]{1,0:T(8,128)(2,1)} %wp_hbm.1, ...), custom_call_target="tpu_custom_call" | custom-call | tf_op jit(solution)/shard_map/pallas_call | solution.py:386
  27.9 1.0 %shard_map.86 = (bf16[128,1024]{1,0:T(8,128)(2,1)}, bf16[128,256]{1,0:T(8,128)(2,1)}, bf16[128,64]{1,0:T(8,128)(2,1)}) custom-call(bf16[1024,128]{1,0:T(8,128)(2,1)S(1)} %bitcast.7, bf16[128,256]{1,0:T(8,128)(2,1)S(1)} %get-tuple-element.10.query, f32[128,128]{1,0:T(8,128)S(1)} %get-tuple-element.11.offset_ref), custom_call_target="tpu_custom_call" | custom-call | tf_op jit(solution)/shard_map/pallas_call | solution.py:432

commit v7 on v5

--- a/solution.py
+++ b/solution.py
@@ -31,8 +31,8 @@
     w1, w2, wp, bias,
     tiles, edge_rows, edge_out, edge_in,
     grid, patches, conv, hidden, patches2, conv2,
-    stats, pool_a,
-    in_sem, row_send, row_recv, edge_send, edge_recv, all_send, all_recv, key_recv,
+    pairs, stats, pool_a,
+    in_sem, row_send, row_recv, edge_send, edge_recv, all_send, all_recv, key_recv, pair_send, pair_recv,
 ):
     tr = lax.axis_index("tr")
     tc = lax.axis_index("tc")
@@ -176,22 +176,46 @@
     def middle(weights):
         return jnp.concatenate([weights[384:1152], weights[0:768]], axis=1)
 
-    def send_block(slots, phase):
-        each(lambda index: pltpu.make_async_remote_copy(
-            src_ref=slots.at[me], dst_ref=slots.at[me],
-            send_sem=all_send.at[phase], recv_sem=all_recv.at[phase],
-            device_id=index, device_id_type=FLAT,
-        ).start(), far_first)
-
-    def arrived(slots, sem):
-        others = slots.at[pl.ds(0, devices - 1)]
-        pltpu.make_async_copy(others, others, sem).wait()
+    core = lax.rem(tc, 2)
+    sibling = jnp.where(core == 0, me + 1, me - 1)
+    chips = devices // 2
+    chip = me // 2
+    far_chips = sorted(range(1, chips), key=lambda h: -min(h, chips - h))
+
+    def each_chip(act, order):
+        def turn(hop, carried=0):
+            act(hop)
+            return carried
+
+        if chips <= 16:
+            for hop in order:
+                turn(hop)
+        else:
+            lax.fori_loop(1, chips, turn, 0)
 
     def share(upper, lower, phase):
         total = jnp.sum(upper + lower, axis=0, keepdims=True)
         squares = jnp.sum(upper * upper + lower * lower, axis=0, keepdims=True)
-        stats[phase, me] = jnp.concatenate([total, squares], axis=0)
-        send_block(stats.at[phase], phase)
+        pairs[phase, core] = jnp.concatenate([total, squares], axis=0)
+        pltpu.make_async_remote_copy(
+            src_ref=pairs.at[phase, core], dst_ref=pairs.at[phase, core],
+            send_sem=pair_send.at[phase], recv_sem=pair_recv.at[phase],
+            device_id=sibling, device_id_type=FLAT,
+        ).start()
+
+    def pass_on(phase):
+        one = pairs.at[phase, 0]
+        pltpu.make_async_copy(one, one, pair_recv.at[phase]).wait()
+        stats[phase, chip] = pairs[phase, 0] + pairs[phase, 1]
+        each_chip(lambda hop: pltpu.make_async_remote_copy(
+            src_ref=stats.at[phase, chip], dst_ref=stats.at[phase, chip],
+            send_sem=all_send.at[phase], recv_sem=all_recv.at[phase],
+            device_id=wrap(me + 2 * hop), device_id_type=FLAT,
+        ).start(), far_chips)
+
+    def arrived(slots, sem):
+        others = slots.at[pl.ds(0, chips - 1)]
+        pltpu.make_async_copy(others, others, sem).wait()
 
     def collect(phase):
         arrived(stats.at[phase], all_recv.at[phase])
@@ -260,26 +284,27 @@
         await_edge(corner)
     finish_own(1, both)
     both = start_own(0)
+    pass_on(1)
     for line in lines[:2]:
         await_row(0, line)
     finish_own(0, both)
     for line in lines[2:]:
         await_row(1, line)
     edge_lines(1)
+    pass_on(0)
     loads[3].wait()
     second_half(1)
     for line in lines[2:]:
         await_row(0, line)
     edge_lines(0)
+    pass_on(3)
     second_half(0)
+    pass_on(2)
     block = blocks_of(1)
 
     pool_a[0:cols, :] = block[0].astype(F32) + block[1].astype(F32)
     small = (pool_a[pl.ds(0, pooled_cols, stride=2), :] + pool_a[pl.ds(1, pooled_cols, stride=2), :]) * 0.25
     keys[me] = small.astype(BF16)
-    sibling = jnp.where(lax.rem(tc, 2) == 0, me + 1, me - 1)
-    chips = devices // 2
-
     def hand_over(block):
         pltpu.make_async_remote_copy(
             src_ref=keys.at[block], dst_ref=keys.at[block],
@@ -299,18 +324,6 @@
         pltpu.make_async_copy(keys.at[block], keys.at[block], key_recv.at[hop]).wait()
         hand_over(block)
 
-    def each_chip(act, order):
-        def turn(hop, carried=0):
-            act(hop)
-            return carried
-
-        if chips <= 16:
-            for hop in order:
-                turn(hop)
-        else:
-            lax.fori_loop(1, chips, turn, 0)
-
-    far_chips = sorted(range(1, chips), key=lambda h: -min(h, chips - h))
     each_chip(send_key, far_chips)
     hand_over(me)
 
@@ -347,6 +360,8 @@
 
     for phase in range(4):
         arrived(stats.at[phase], all_send.at[phase])
+        one = pairs.at[phase, 0]
+        pltpu.make_async_copy(one, one, pair_send.at[phase]).wait()
     sent = keys.at[pl.ds(0, chips - 1)]
     pltpu.make_async_copy(sent, sent, all_send.at[4]).wait()
     pltpu.make_async_copy(handed, handed, all_send.at[5]).wait()
@@ -416,7 +431,8 @@
             vmem((2, 4, cols + 32, cin), F32),
             vmem((2, 4, cols, 3 * cin), BF16),
             vmem((2, rows, cols, cin), F32),
-            vmem((4, devices, 2, cin), F32),
+            vmem((4, 2, 2, cin), F32),
+            vmem((4, devices // 2, 2, cin), F32),
             vmem((cols, cin), F32),
             pltpu.SemaphoreType.DMA((6,)),
             pltpu.SemaphoreType.DMA((4, 2)),
@@ -426,6 +442,8 @@
             pltpu.SemaphoreType.DMA((6,)),
             pltpu.SemaphoreType.DMA((6,)),
             pltpu.SemaphoreType.DMA((devices // 2,)),
+            pltpu.SemaphoreType.DMA((4,)),
+            pltpu.SemaphoreType.DMA((4,)),
         ],
         compiler_params=pltpu.CompilerParams(
             collective_id=0, has_side_effects=True, vmem_limit_bytes=48 * 1024 * 1024

time: 28.8 us -> 29.5 us (1.024)
  Pallas kernels: 28.1 us -> 28.8 us
    pallas_call x1, Pallas kernels: 27 us -> 27.7 us  [body(): pl.pallas_call(functools.partial(kernel, row_tiles, col_tiles, rows, cols...]
where the time goes in v7:
time: 29.5 us; the launch traced here: 29.4 us
  Pallas kernels  28.8 us (98%)
  between operations  0.64 us (2%)
    pallas_call x1, Pallas kernels, body(): pl.pallas_call(functools.partial(kernel, row_tiles, col_tiles, rows, cols...  27.7 us
    pallas_call x1, Pallas kernels, body(): pl.pallas_call(functools.partial(correlate, col_tiles * cols // 2), out_s...  1.04 us

profile of v7, /device:TPU:0, one launch (start us, length us, event | category | flops | bytes accessed | tf_op | source)
XLA Modules:
  0.0 29.4 jit_solution(14069138400000274203)
XLA Ops:
  0.6 27.7 %shard_map.85 = (bf16[32,32,128]{2,1,0:T(8,128)(2,1)S(1)}, bf16[128,256]{1,0:T(8,128)(2,1)S(1)}, f32[128,128]{1,0:T(8,128)S(1)}) custom-call(bf16[2,64,128]{2,1,0:T(8,128)(2,1)} %f1.1, bf16[2,64,128]{2,1,0:T(8,128)(2,1)} %f2.1, bf16[1152,128]{1,0:T(8,128)(2,1)} %bitcast.8, bf16[1152,128]{1,0:T(8,128)(2,1)} %bitcast.9, bf16[128,256]{1,0:T(8,128)(2,1)} %wp_hbm.1, ...), custom_call_target="tpu_custom_call" | custom-call | tf_op jit(solution)/shard_map/pallas_call | solution.py:410
  28.4 1.0 %shard_map.86 = (bf16[128,1024]{1,0:T(8,128)(2,1)}, bf16[128,256]{1,0:T(8,128)(2,1)}, bf16[128,64]{1,0:T(8,128)(2,1)}) custom-call(bf16[1024,128]{1,0:T(8,128)(2,1)S(1)} %bitcast.7, bf16[128,256]{1,0:T(8,128)(2,1)S(1)} %get-tuple-element.10.query, f32[128,128]{1,0:T(8,128)S(1)} %get-tuple-element.11.offset_ref), custom_call_target="tpu_custom_call" | custom-call | tf_op jit(solution)/shard_map/pallas_call | solution.py:459

commit v8 on v5

--- a/solution.py
+++ b/solution.py
@@ -147,10 +147,8 @@
 
     for corner in corners:
         send_edge(corner)
-    for pair in (lines[:2], lines[2:]):
-        for f in (1, 0):
-            for line in pair:
-                send_row(f, line)
+    for line in lines:
+        send_row(1, line)
 
     wide = cols + 16
 
@@ -259,19 +257,20 @@
     for corner in corners[2:]:
         await_edge(corner)
     finish_own(1, both)
+    for line in lines:
+        send_row(0, line)
     both = start_own(0)
-    for line in lines[:2]:
-        await_row(0, line)
-    finish_own(0, both)
     for line in lines[2:]:
         await_row(1, line)
     edge_lines(1)
     loads[3].wait()
     second_half(1)
+    for line in lines[:2]:
+        await_row(0, line)
+    finish_own(0, both)
     for line in lines[2:]:
         await_row(0, line)
     edge_lines(0)
-    second_half(0)
     block = blocks_of(1)
 
     pool_a[0:cols, :] = block[0].astype(F32) + block[1].astype(F32)
@@ -313,6 +312,7 @@
     far_chips = sorted(range(1, chips), key=lambda h: -min(h, chips - h))
     each_chip(send_key, far_chips)
     hand_over(me)
+    second_half(0)
 
     loads[4].wait()
     loads[5].wait()

time: 28.8 us -> 29.4 us (1.021)
  Pallas kernels: 28.1 us -> 28.6 us
    pallas_call x1, Pallas kernels: 27 us -> 27.6 us  [body(): pl.pallas_call(functools.partial(kernel, row_tiles, col_tiles, rows, cols...]
where the time goes in v8:
time: 29.4 us; the launch traced here: 29.3 us
  Pallas kernels  28.6 us (97%)
  between operations  0.64 us (2%)
    pallas_call x1, Pallas kernels, body(): pl.pallas_call(functools.partial(kernel, row_tiles, col_tiles, rows, cols...  27.6 us
    pallas_call x1, Pallas kernels, body(): pl.pallas_call(functools.partial(correlate, col_tiles * cols // 2), out_s...  1.04 us

profile of v8, /device:TPU:0, one launch (start us, length us, event | category | flops | bytes accessed | tf_op | source)
XLA Modules:
  0.0 29.3 jit_solution(14024627066939351264)
XLA Ops:
  0.6 27.6 %shard_map.85 = (bf16[32,32,128]{2,1,0:T(8,128)(2,1)S(1)}, bf16[128,256]{1,0:T(8,128)(2,1)S(1)}, f32[128,128]{1,0:T(8,128)S(1)}) custom-call(bf16[2,64,128]{2,1,0:T(8,128)(2,1)} %f1.1, bf16[2,64,128]{2,1,0:T(8,128)(2,1)} %f2.1, bf16[1152,128]{1,0:T(8,128)(2,1)} %bitcast.8, bf16[1152,128]{1,0:T(8,128)(2,1)} %bitcast.9, bf16[128,256]{1,0:T(8,128)(2,1)} %wp_hbm.1, ...), custom_call_target="tpu_custom_call" | custom-call | tf_op jit(solution)/shard_map/pallas_call | solution.py:395
  28.2 1.0 %shard_map.86 = (bf16[128,1024]{1,0:T(8,128)(2,1)}, bf16[128,256]{1,0:T(8,128)(2,1)}, bf16[128,64]{1,0:T(8,128)(2,1)}) custom-call(bf16[1024,128]{1,0:T(8,128)(2,1)S(1)} %bitcast.7, bf16[128,256]{1,0:T(8,128)(2,1)S(1)} %get-tuple-element.10.query, f32[128,128]{1,0:T(8,128)S(1)} %get-tuple-element.11.offset_ref), custom_call_target="tpu_custom_call" | custom-call | tf_op jit(solution)/shard_map/pallas_call | solution.py:441
